TPU v7x, 512 devices: a whole 4x8x8 slice. The times are simulated.
512 devices in a mesh: head: 8 (over y_hi, core), ctx: 64 (over y_lo, z, x).
Axes of the slice: x: 4, y: 8 (y_hi: 4, y_lo: 2; y = y_hi * 2 + y_lo), z: 8, core: 2. Of those that a mesh axis runs over, the one named last changes fastest.
Arguments:
- queries: bfloat16 [32768, 4096], P(('head', 'ctx')), may hold values from -6 to 6
- keys: bfloat16 [32768, 4096], P(('head', 'ctx')), may hold values from -6 to 6
- values: bfloat16 [32768, 4096], P(('head', 'ctx')), may hold values from -6 to 6
- outputs: bfloat16 [32768, 4096], P(('head', 'ctx')), may hold values from -6 to 6
- grad_out: bfloat16 [32768, 4096], P(('head', 'ctx')), may hold values from -235 to 235
- log_totals: float32 [32768, 32], P(('head', 'ctx')), may hold values from 0 to 20
- pair_live: int32 [2, 64], replicated, may hold values from 0 to 1, as said below
Outputs:
- grad_queries: bfloat16 [32768, 4096], P(('head', 'ctx'))
- grad_keys: bfloat16 [32768, 4096], P(('head', 'ctx'))
- grad_values: bfloat16 [32768, 4096], P(('head', 'ctx'))
Inputs may be any that keep to these rules, and one draw needn't show every extreme that they name: pair_live[r, c] equals pair_live[r, c XOR (64 / 2^(r + 1))]; in every round some pairs are live and some are not.
All inputs are finite; a program needn't handle non-finite values.
Results may differ from a plain program's by a relative error of at most 0.0065.
Values may be sent and summed in bfloat16 or wider, within the bound.
A program may use at most 64 MiB of HBM per device.

v0:
```python
import jax
import jax.numpy as jnp
from jax import lax
from jax.sharding import PartitionSpec as P

H = 32
HD = 128
ROUNDS = 2


def swapped(array, axis, distance):
    return lax.ppermute(array, axis, [(i, i ^ 1 << distance) for i in range(lax.axis_size(axis))])


def pair_terms(qb, dob, lseb, deltab, kb, vb):
    scale = 1.0 / qb.shape[-1] ** 0.5
    scores = jnp.einsum("qhd,khd->hqk", qb, kb, preferred_element_type=jnp.float32) * scale
    probs = jnp.exp(scores - jnp.transpose(lseb)[:, :, None])
    probs_b = probs.astype(jnp.bfloat16)
    grad_v = jnp.einsum("hqk,qhd->khd", probs_b, dob, preferred_element_type=jnp.float32)
    grad_p = jnp.einsum("qhd,khd->hqk", dob, vb, preferred_element_type=jnp.float32)
    grad_s = (probs * (grad_p - jnp.transpose(deltab)[:, :, None])).astype(jnp.bfloat16)
    grad_q = jnp.einsum("hqk,khd->qhd", grad_s, kb, preferred_element_type=jnp.float32) * scale
    grad_k = jnp.einsum("hqk,qhd->khd", grad_s, qb, preferred_element_type=jnp.float32) * scale
    return (grad_q, grad_k, grad_v)


def on_device(queries, keys, values, outputs, grad_out, log_totals, pair_live):
    heads_local = H // lax.axis_size("head")
    q_flat, k_flat, v_flat, o_flat, do_flat = (
        lax.all_to_all(queries, "head", split_axis=1, concat_axis=0, tiled=True),
        lax.all_to_all(keys, "head", split_axis=1, concat_axis=0, tiled=True),
        lax.all_to_all(values, "head", split_axis=1, concat_axis=0, tiled=True),
        lax.all_to_all(outputs, "head", split_axis=1, concat_axis=0, tiled=True),
        lax.all_to_all(grad_out, "head", split_axis=1, concat_axis=0, tiled=True),
    )
    lse_block = lax.all_to_all(log_totals, "head", split_axis=1, concat_axis=0, tiled=True)
    delta_block = jnp.sum(
        (do_flat.astype(jnp.float32) * o_flat.astype(jnp.float32)).reshape(-1, heads_local, HD),
        axis=-1,
    )
    block_rows = q_flat.shape[0]
    q_heads = q_flat.reshape(block_rows, heads_local, HD)
    k_heads = k_flat.reshape(block_rows, heads_local, HD)
    v_heads = v_flat.reshape(block_rows, heads_local, HD)
    do_heads = do_flat.reshape(block_rows, heads_local, HD)
    grad_q, grad_k, grad_v = pair_terms(q_heads, do_heads, lse_block, delta_block, k_heads, v_heads)
    zero_heads = jnp.zeros((block_rows, heads_local, HD), jnp.float32)
    ctx_place = lax.axis_index("ctx")
    top_bit = lax.axis_size("ctx").bit_length() - 1
    for step in range(ROUNDS):
        bit = top_bit - 1 - step
        live = pair_live[step, ctx_place] > 0
        other_k, other_v = swapped((k_heads, v_heads), "ctx", bit)
        terms = lax.cond(
            live,
            lambda: pair_terms(q_heads, do_heads, lse_block, delta_block, other_k, other_v),
            lambda: (zero_heads, zero_heads, zero_heads),
        )
        grad_q = grad_q + terms[0]
        back_k, back_v = swapped((terms[1], terms[2]), "ctx", bit)
        grad_k = grad_k + back_k
        grad_v = grad_v + back_v
    width = heads_local * HD
    rounded_q = grad_q.astype(jnp.bfloat16).reshape(block_rows, width)
    rounded_k = grad_k.astype(jnp.bfloat16).reshape(block_rows, width)
    rounded_v = grad_v.astype(jnp.bfloat16).reshape(block_rows, width)
    return (
        lax.all_to_all(rounded_q, "head", split_axis=0, concat_axis=1, tiled=True),
        lax.all_to_all(rounded_k, "head", split_axis=0, concat_axis=1, tiled=True),
        lax.all_to_all(rounded_v, "head", split_axis=0, concat_axis=1, tiled=True),
    )


def solution(mesh):
    return jax.shard_map(
        on_device,
        mesh=mesh,
        in_specs=(
            P(("head", "ctx"), None),
            P(("head", "ctx"), None),
            P(("head", "ctx"), None),
            P(("head", "ctx"), None),
            P(("head", "ctx"), None),
            P(("head", "ctx"), None),
            P(),
        ),
        out_specs=(P(("head", "ctx"), None), P(("head", "ctx"), None), P(("head", "ctx"), None)),
        check_vma=False,
    )
```

profile of v0, /device:TPU:8, one launch (start us, length us, event | category | flops | bytes accessed | tf_op | source)
XLA Modules:
  0.0 305.3 jit_solution(14661163394751335364)
XLA Ops:
  2.1 6.2 %all-to-all-start.2 = ((f32[8,1,256]{2,1,0:T(1,128)}), f32[8,1,256]{2,1,0:T(1,128)S(1)}, u32[]{:S(2)}, u32[]{:S(2)}) async-start(f32[8,1,256]{2,1,0:T(1,128)} %reshape.81), calls=%async_computation.2 | async-start | bytes 16384 | tf_op jit(solution)/shard_map/all_to_all | solution.py:37
  10.3 5.8 %all-to-all-done.2 = f32[8,1,256]{2,1,0:T(1,128)S(1)} async-done(((f32[8,1,256]{2,1,0:T(1,128)}), f32[8,1,256]{2,1,0:T(1,128)S(1)}, u32[]{:S(2)}, u32[]{:S(2)}) %all-to-all-start.2) | async-done | bytes 8224 | tf_op jit(solution)/shard_map/all_to_all | solution.py:37
  16.1 3.5 %all-to-all-start.3 = ((bf16[64,8,512]{2,0,1:T(8,128)(2,1)}), bf16[64,8,512]{2,0,1:T(8,128)(2,1)S(1)}, u32[]{:S(2)}, u32[]{:S(2)}) async-start(bf16[64,8,512]{2,0,1:T(8,128)(2,1)} %bitcast.72), calls=%async_computation.3 | async-start | bytes 1048576 | tf_op jit(solution)/shard_map/all_to_all | solution.py:35
  21.5 16.4 %all-to-all-done.3 = bf16[64,8,512]{2,0,1:T(8,128)(2,1)S(1)} async-done(((bf16[64,8,512]{2,0,1:T(8,128)(2,1)}), bf16[64,8,512]{2,0,1:T(8,128)(2,1)S(1)}, u32[]{:S(2)}, u32[]{:S(2)}) %all-to-all-start.3) | async-done | bytes 524320 | tf_op jit(solution)/shard_map/all_to_all | solution.py:35
  37.9 3.5 %all-to-all-start.5 = ((bf16[64,8,512]{2,0,1:T(8,128)(2,1)}), bf16[64,8,512]{2,0,1:T(8,128)(2,1)S(1)}, u32[]{:S(2)}, u32[]{:S(2)}) async-start(bf16[64,8,512]{2,0,1:T(8,128)(2,1)} %bitcast.70), calls=%async_computation.5 | async-start | bytes 1048576 | tf_op jit(solution)/shard_map/all_to_all | solution.py:34
  42.2 16.8 %all-to-all-done.5 = bf16[64,8,512]{2,0,1:T(8,128)(2,1)S(1)} async-done(((bf16[64,8,512]{2,0,1:T(8,128)(2,1)}), bf16[64,8,512]{2,0,1:T(8,128)(2,1)S(1)}, u32[]{:S(2)}, u32[]{:S(2)}) %all-to-all-start.5) | async-done | bytes 524320 | tf_op jit(solution)/shard_map/all_to_all | solution.py:34
  59.0 3.5 %all-to-all-start.1 = ((bf16[64,8,512]{2,0,1:T(8,128)(2,1)}), bf16[64,8,512]{2,0,1:T(8,128)(2,1)S(1)}, u32[]{:S(2)}, u32[]{:S(2)}) async-start(bf16[64,8,512]{2,0,1:T(8,128)(2,1)} %bitcast.73), calls=%async_computation.1 | async-start | bytes 1048576 | tf_op jit(solution)/shard_map/all_to_all | solution.py:32
  63.3 15.9 %all-to-all-done.1 = bf16[64,8,512]{2,0,1:T(8,128)(2,1)S(1)} async-done(((bf16[64,8,512]{2,0,1:T(8,128)(2,1)}), bf16[64,8,512]{2,0,1:T(8,128)(2,1)S(1)}, u32[]{:S(2)}, u32[]{:S(2)}) %all-to-all-start.1) | async-done | bytes 524320 | tf_op jit(solution)/shard_map/all_to_all | solution.py:32
  83.6 17.4 %all-to-all-done.4 = bf16[64,8,512]{2,0,1:T(8,128)(2,1)S(1)} async-done(((bf16[64,8,512]{2,0,1:T(8,128)(2,1)}), bf16[64,8,512]{2,0,1:T(8,128)(2,1)S(1)}, u32[]{:S(2)}, u32[]{:S(2)}) %all-to-all-start.4) | async-done | bytes 524320 | tf_op jit(solution)/shard_map/all_to_all | solution.py:33
  101.1 4.1 %all-to-all-start = ((bf16[64,8,512]{2,0,1:T(8,128)(2,1)}), bf16[64,8,512]{2,0,1:T(8,128)(2,1)}, u32[]{:S(2)}, u32[]{:S(2)}) async-start(bf16[64,8,512]{2,0,1:T(8,128)(2,1)} %bitcast.74), calls=%async_computation | async-start | bytes 1048576 | tf_op jit(solution)/shard_map/all_to_all | solution.py:31
  112.0 12.4 %collective-permute-start.2 = (bf16[512,4,128]{2,1,0:T(4,128)(2,1)}, bf16[512,4,128]{2,1,0:T(4,128)(2,1)}, u32[]{:S(2)}, u32[]{:S(2)}) collective-permute-start(bf16[512,4,128]{2,1,0:T(4,128)(2,1)} %reshape.75), channel_id=1, source_target_pairs={{0,16},{1,17},{2,18},{3,19},{4,20},{5,21},{6,22},{7,23},{8,24},{9,... | collective-permute-start | bytes 1572872 | tf_op jit(solution)/shard_map/ppermute | solution.py:12
  131.8 3.7 %fusion.52 = f32[4,512,512]{2,1,0:T(8,128)} fusion(bf16[512,4,128]{2,1,0:T(4,128)(2,1)} %reshape.75, bf16[512,4,128]{2,1,0:T(4,128)(2,1)S(1)} %reshape.74), kind=kOutput, calls=%fused_computation.65 | convolution fusion | flops 268435456 | bytes 5242880 | tf_op jit(solution)/shard_map/qhd,khd->hqk/dot_general | solution.py:17
  141.5 14.1 %conditional.2 = (f32[512,4,128]{2,0,1:T(8,128)}, f32[512,4,128]{2,0,1:T(8,128)}, f32[512,4,128]{2,0,1:T(8,128)}) conditional(s32[]{:T(128)} %bitcast.20, () %tuple.24, (bf16[512,4,128]{2,1,0:T(4,128)(2,1)S(1)}, bf16[512,4,128]{2,1,0:T(4,128)(2,1)}, f32[512,4]{0,1:T(4,128)S(1)}, bf16[512,4,128]{2,1,0:T(4,128)(2,1)S(1)}, ...), branch_computations={%region_1.0_spmd, %region_2.0_spmd} | conditional | flops 1351090176 | bytes 42508340 | solution.py:55
  141.5 3.8 %fusion.13 = f32[4,512,512]{2,1,0:T(8,128)} fusion(bf16[512,4,128]{2,1,0:T(4,128)(2,1)} %get-tuple-element.88, bf16[512,4,128]{2,1,0:T(4,128)(2,1)S(1)} %get-tuple-element.87), kind=kOutput, calls=%fused_computation.14 | convolution fusion | flops 268435456 | bytes 5242880 | tf_op jit(solution)/shard_map/cond/branch_1_fun/qhd,khd->hqk/dot_general | solution.py:17
  158.5 14.4 %conditional.3 = (f32[512,4,128]{2,0,1:T(8,128)}, f32[512,4,128]{2,0,1:T(8,128)}, f32[512,4,128]{2,0,1:T(8,128)}) conditional(s32[]{:T(128)} %bitcast.21, () %tuple.26, (bf16[512,4,128]{2,1,0:T(4,128)(2,1)S(1)}, bf16[512,4,128]{2,1,0:T(4,128)(2,1)}, f32[512,4]{0,1:T(4,128)S(1)}, bf16[512,4,128]{2,1,0:T(4,128)(2,1)S(1)}, ...), branch_computations={%region_3.0_spmd, %region_4.0_spmd} | conditional | flops 1351090176 | bytes 42508340 | solution.py:55
  158.7 3.8 %fusion.32 = f32[4,512,512]{2,1,0:T(8,128)} fusion(bf16[512,4,128]{2,1,0:T(4,128)(2,1)} %get-tuple-element.94, bf16[512,4,128]{2,1,0:T(4,128)(2,1)S(1)} %get-tuple-element.93), kind=kOutput, calls=%fused_computation.34 | convolution fusion | flops 268435456 | bytes 5242880 | tf_op jit(solution)/shard_map/cond/branch_1_fun/qhd,khd->hqk/dot_general | solution.py:17
  172.9 19.4 %collective-permute-start.5 = (f32[512,4,128]{2,0,1:T(8,128)}, f32[512,4,128]{2,0,1:T(8,128)}, u32[]{:S(2)}, u32[]{:S(2)}) collective-permute-start(f32[512,4,128]{2,0,1:T(8,128)} %get-tuple-element.48), channel_id=1, source_target_pairs={{0,16},{1,17},{2,18},{3,19},{4,20},{5,21},{6,22},{7,23},{8,24},{9,... | collective-permute-start | bytes 3145736 | tf_op jit(solution)/shard_map/ppermute | solution.py:12
  199.0 6.9 %all-to-all-start.6 = ((bf16[8,64,512]{2,1,0:T(8,128)(2,1)}), bf16[8,64,512]{2,1,0:T(8,128)(2,1)}, u32[]{:S(2)}, u32[]{:S(2)}) async-start(bf16[8,64,512]{2,1,0:T(8,128)(2,1)} %all_to_all.132), calls=%async_computation.6 | async-start | bytes 1048576 | tf_op jit(solution)/shard_map/all_to_all | solution.py:69
  211.4 37.9 %collective-permute-done.5 = f32[512,4,128]{2,0,1:T(8,128)} collective-permute-done((f32[512,4,128]{2,0,1:T(8,128)}, f32[512,4,128]{2,0,1:T(8,128)}, u32[]{:S(2)}, u32[]{:S(2)}) %collective-permute-start.5) | collective-permute-done | bytes 1048608 | tf_op jit(solution)/shard_map/ppermute | solution.py:12
  252.5 6.8 %all-to-all-start.7 = ((bf16[8,64,512]{2,1,0:T(8,128)(2,1)}), bf16[8,64,512]{2,1,0:T(8,128)(2,1)S(1)}, u32[]{:S(2)}, u32[]{:S(2)}) async-start(bf16[8,64,512]{2,1,0:T(8,128)(2,1)} %all_to_all.136), calls=%async_computation.7 | async-start | bytes 1048576 | tf_op jit(solution)/shard_map/all_to_all | solution.py:70
  259.4 3.5 %fusion.43 = f32[512,4,128]{2,0,1:T(8,128)S(1)} fusion(f32[4,512,512]{2,1,0:T(8,128)} %fusion.52, f32[4,512]{1,0:T(4,128)S(1)} %bitcast.90, bf16[512,4,128]{2,1,0:T(4,128)(2,1)S(1)} %reshape.76), kind=kOutput, calls=%fused_computation.46 | convolution fusion | flops 271581184 | bytes 5775360 | tf_op jit(solution)/shard_map/hqk,qhd->khd/dot_general | solution.py:20
  262.9 13.7 %collective-permute-done.7 = f32[512,4,128]{2,0,1:T(8,128)} collective-permute-done((f32[512,4,128]{2,0,1:T(8,128)}, f32[512,4,128]{2,0,1:T(8,128)}, u32[]{:S(2)}, u32[]{:S(2)}) %collective-permute-start.7) | collective-permute-done | bytes 1048608 | tf_op jit(solution)/shard_map/ppermute | solution.py:12
  279.7 6.9 %all-to-all-start.8 = ((bf16[8,64,512]{2,1,0:T(8,128)(2,1)}), bf16[8,64,512]{2,1,0:T(8,128)(2,1)S(1)}, u32[]{:S(2)}, u32[]{:S(2)}) async-start(bf16[8,64,512]{2,1,0:T(8,128)(2,1)} %all_to_all.140), calls=%async_computation.8 | async-start | bytes 1048576 | tf_op jit(solution)/shard_map/all_to_all | solution.py:71
  289.3 15.1 %all-to-all-done.8 = bf16[8,64,512]{2,1,0:T(8,128)(2,1)S(1)} async-done(((bf16[8,64,512]{2,1,0:T(8,128)(2,1)}), bf16[8,64,512]{2,1,0:T(8,128)(2,1)S(1)}, u32[]{:S(2)}, u32[]{:S(2)}) %all-to-all-start.8) | async-done | bytes 524320 | tf_op jit(solution)/shard_map/all_to_all | solution.py:71
  (74 shorter events, 75.8 us)
Async XLA Ops:
  0.6 40.7 %copy-start.2 = (bf16[64,4096]{1,0:T(8,128)(2,1)S(1)}, bf16[64,4096]{1,0:T(8,128)(2,1)}, u32[]{:S(2)}) copy-start(bf16[64,4096]{1,0:T(8,128)(2,1)} %param.12) | copy-start | bytes 1572868
  0.6 61.9 %copy-start.3 = (bf16[64,4096]{1,0:T(8,128)(2,1)S(1)}, bf16[64,4096]{1,0:T(8,128)(2,1)}, u32[]{:S(2)}) copy-start(bf16[64,4096]{1,0:T(8,128)(2,1)} %param.13) | copy-start | bytes 1572868
  2.1 13.9 %all-to-all-start.2 = ((f32[8,1,256]{2,1,0:T(1,128)}), f32[8,1,256]{2,1,0:T(1,128)S(1)}, u32[]{:S(2)}, u32[]{:S(2)}) async-start(f32[8,1,256]{2,1,0:T(1,128)} %reshape.81), calls=%async_computation.2 | async-start | bytes 16384 | tf_op jit(solution)/shard_map/all_to_all | solution.py:37
  8.3 74.4 %copy-start.4 = (bf16[64,4096]{1,0:T(8,128)(2,1)S(1)}, bf16[64,4096]{1,0:T(8,128)(2,1)}, u32[]{:S(2)}) copy-start(bf16[64,4096]{1,0:T(8,128)(2,1)} %param.11) | copy-start | bytes 1572868
  16.1 21.8 %all-to-all-start.3 = ((bf16[64,8,512]{2,0,1:T(8,128)(2,1)}), bf16[64,8,512]{2,0,1:T(8,128)(2,1)S(1)}, u32[]{:S(2)}, u32[]{:S(2)}) async-start(bf16[64,8,512]{2,0,1:T(8,128)(2,1)} %bitcast.72), calls=%async_computation.3 | async-start | bytes 1048576 | tf_op jit(solution)/shard_map/all_to_all | solution.py:35
  19.6 85.6 %copy-start.5 = (s32[2,64]{1,0:T(2,128)S(1)}, s32[2,64]{1,0:T(2,128)}, u32[]{:S(2)}) copy-start(s32[2,64]{1,0:T(2,128)} %param.17) | copy-start | bytes 1540
  37.9 21.1 %all-to-all-start.5 = ((bf16[64,8,512]{2,0,1:T(8,128)(2,1)}), bf16[64,8,512]{2,0,1:T(8,128)(2,1)S(1)}, u32[]{:S(2)}, u32[]{:S(2)}) async-start(bf16[64,8,512]{2,0,1:T(8,128)(2,1)} %bitcast.70), calls=%async_computation.5 | async-start | bytes 1048576 | tf_op jit(solution)/shard_map/all_to_all | solution.py:34
  59.0 20.3 %all-to-all-start.1 = ((bf16[64,8,512]{2,0,1:T(8,128)(2,1)}), bf16[64,8,512]{2,0,1:T(8,128)(2,1)S(1)}, u32[]{:S(2)}, u32[]{:S(2)}) async-start(bf16[64,8,512]{2,0,1:T(8,128)(2,1)} %bitcast.73), calls=%async_computation.1 | async-start | bytes 1048576 | tf_op jit(solution)/shard_map/all_to_all | solution.py:32
  79.3 21.8 %all-to-all-start.4 = ((bf16[64,8,512]{2,0,1:T(8,128)(2,1)}), bf16[64,8,512]{2,0,1:T(8,128)(2,1)S(1)}, u32[]{:S(2)}, u32[]{:S(2)}) async-start(bf16[64,8,512]{2,0,1:T(8,128)(2,1)} %bitcast.71), calls=%async_computation.4 | async-start | bytes 1048576 | tf_op jit(solution)/shard_map/all_to_all | solution.py:33
  101.1 29.6 %all-to-all-start = ((bf16[64,8,512]{2,0,1:T(8,128)(2,1)}), bf16[64,8,512]{2,0,1:T(8,128)(2,1)}, u32[]{:S(2)}, u32[]{:S(2)}) async-start(bf16[64,8,512]{2,0,1:T(8,128)(2,1)} %bitcast.74), calls=%async_computation | async-start | bytes 1048576 | tf_op jit(solution)/shard_map/all_to_all | solution.py:31
  109.4 30.0 %collective-permute-start = (bf16[512,4,128]{2,1,0:T(4,128)(2,1)}, bf16[512,4,128]{2,1,0:T(4,128)(2,1)}, u32[]{:S(2)}, u32[]{:S(2)}) collective-permute-start(bf16[512,4,128]{2,1,0:T(4,128)(2,1)} %reshape.75), channel_id=1, source_target_pairs={{0,32},{1,33},{2,34},{3,35},{4,36},{5,37},{6,38},{7,39},{8,40},{9,... | collective-permute-start | bytes 1572872 | tf_op jit(solution)/shard_map/ppermute | solution.py:12
  112.0 46.5 %collective-permute-start.2 = (bf16[512,4,128]{2,1,0:T(4,128)(2,1)}, bf16[512,4,128]{2,1,0:T(4,128)(2,1)}, u32[]{:S(2)}, u32[]{:S(2)}) collective-permute-start(bf16[512,4,128]{2,1,0:T(4,128)(2,1)} %reshape.75), channel_id=1, source_target_pairs={{0,16},{1,17},{2,18},{3,19},{4,20},{5,21},{6,22},{7,23},{8,24},{9,... | collective-permute-start | bytes 1572872 | tf_op jit(solution)/shard_map/ppermute | solution.py:12
  125.3 16.1 %collective-permute-start.1 = (bf16[512,4,128]{2,1,0:T(4,128)(2,1)}, bf16[512,4,128]{2,1,0:T(4,128)(2,1)}, u32[]{:S(2)}, u32[]{:S(2)}) collective-permute-start(bf16[512,4,128]{2,1,0:T(4,128)(2,1)} %reshape.77), channel_id=1, source_target_pairs={{0,32},{1,33},{2,34},{3,35},{4,36},{5,37},{6,38},{7,39},{8,40},{9,... | collective-permute-start | bytes 1572872 | tf_op jit(solution)/shard_map/ppermute | solution.py:12
  128.1 30.5 %collective-permute-start.3 = (bf16[512,4,128]{2,1,0:T(4,128)(2,1)}, bf16[512,4,128]{2,1,0:T(4,128)(2,1)}, u32[]{:S(2)}, u32[]{:S(2)}) collective-permute-start(bf16[512,4,128]{2,1,0:T(4,128)(2,1)} %reshape.77), channel_id=1, source_target_pairs={{0,16},{1,17},{2,18},{3,19},{4,20},{5,21},{6,22},{7,23},{8,24},{9,... | collective-permute-start | bytes 1572872 | tf_op jit(solution)/shard_map/ppermute | solution.py:12
  148.4 4.7 %copy-start = (f32[4,512,512]{2,1,0:T(8,128)S(1)}, f32[4,512,512]{2,1,0:T(8,128)}, u32[]{:S(2)}) copy-start(f32[4,512,512]{2,1,0:T(8,128)} %fusion.13) | copy-start | bytes 12582916 | tf_op jit(solution)/shard_map/cond
  155.6 55.9 %collective-permute-start.4 = (f32[512,4,128]{2,0,1:T(8,128)}, f32[512,4,128]{2,0,1:T(8,128)}, u32[]{:S(2)}, u32[]{:S(2)}) collective-permute-start(f32[512,4,128]{2,0,1:T(8,128)} %get-tuple-element.47), channel_id=1, source_target_pairs={{0,32},{1,33},{2,34},{3,35},{4,36},{5,37},{6,38},{7,39},{8,40},{9,... | collective-permute-start | bytes 3145736 | tf_op jit(solution)/shard_map/ppermute | solution.py:12
  165.7 4.7 %copy-start.1 = (f32[4,512,512]{2,1,0:T(8,128)S(1)}, f32[4,512,512]{2,1,0:T(8,128)}, u32[]{:S(2)}) copy-start(f32[4,512,512]{2,1,0:T(8,128)} %fusion.32) | copy-start | bytes 12582916 | tf_op jit(solution)/shard_map/cond
  172.9 76.5 %collective-permute-start.5 = (f32[512,4,128]{2,0,1:T(8,128)}, f32[512,4,128]{2,0,1:T(8,128)}, u32[]{:S(2)}, u32[]{:S(2)}) collective-permute-start(f32[512,4,128]{2,0,1:T(8,128)} %get-tuple-element.48), channel_id=1, source_target_pairs={{0,16},{1,17},{2,18},{3,19},{4,20},{5,21},{6,22},{7,23},{8,24},{9,... | collective-permute-start | bytes 3145736 | tf_op jit(solution)/shard_map/ppermute | solution.py:12
  199.0 53.5 %all-to-all-start.6 = ((bf16[8,64,512]{2,1,0:T(8,128)(2,1)}), bf16[8,64,512]{2,1,0:T(8,128)(2,1)}, u32[]{:S(2)}, u32[]{:S(2)}) async-start(bf16[8,64,512]{2,1,0:T(8,128)(2,1)} %all_to_all.132), calls=%async_computation.6 | async-start | bytes 1048576 | tf_op jit(solution)/shard_map/all_to_all | solution.py:69
  205.9 57.0 %collective-permute-start.6 = (f32[512,4,128]{2,0,1:T(8,128)}, f32[512,4,128]{2,0,1:T(8,128)}, u32[]{:S(2)}, u32[]{:S(2)}) collective-permute-start(f32[512,4,128]{2,0,1:T(8,128)} %get-tuple-element.49), channel_id=1, source_target_pairs={{0,32},{1,33},{2,34},{3,35},{4,36},{5,37},{6,38},{7,39},{8,40},{9,... | collective-permute-start | bytes 3145736 | tf_op jit(solution)/shard_map/ppermute | solution.py:12
  208.6 68.0 %collective-permute-start.7 = (f32[512,4,128]{2,0,1:T(8,128)}, f32[512,4,128]{2,0,1:T(8,128)}, u32[]{:S(2)}, u32[]{:S(2)}) collective-permute-start(f32[512,4,128]{2,0,1:T(8,128)} %get-tuple-element.50), channel_id=1, source_target_pairs={{0,16},{1,17},{2,18},{3,19},{4,20},{5,21},{6,22},{7,23},{8,24},{9,... | collective-permute-start | bytes 3145736 | tf_op jit(solution)/shard_map/ppermute | solution.py:12
  252.5 27.2 %all-to-all-start.7 = ((bf16[8,64,512]{2,1,0:T(8,128)(2,1)}), bf16[8,64,512]{2,1,0:T(8,128)(2,1)S(1)}, u32[]{:S(2)}, u32[]{:S(2)}) async-start(bf16[8,64,512]{2,1,0:T(8,128)(2,1)} %all_to_all.136), calls=%async_computation.7 | async-start | bytes 1048576 | tf_op jit(solution)/shard_map/all_to_all | solution.py:70
  279.7 24.7 %all-to-all-start.8 = ((bf16[8,64,512]{2,1,0:T(8,128)(2,1)}), bf16[8,64,512]{2,1,0:T(8,128)(2,1)S(1)}, u32[]{:S(2)}, u32[]{:S(2)}) async-start(bf16[8,64,512]{2,1,0:T(8,128)(2,1)} %all_to_all.140), calls=%async_computation.8 | async-start | bytes 1048576 | tf_op jit(solution)/shard_map/all_to_all | solution.py:71
where the time goes:
time: 309 us; the launch traced here: 305 us
  waiting for transfers between devices  141 us (46%)
  starting transfers between devices  91.5 us (30%)
  matrix products  40.9 us (13%)
  local copies, waits for them, and re-layouts  22.6 us (7%)
  other arithmetic  6.55 us (2%)
    ppermute x8, waiting for transfers between devices, swapped(): lax.ppermute(array, axis, [(i, i ^ 1 << distance) for i in range(lax.axis...  53.8 us
    ppermute x8, starting transfers between devices, swapped(): lax.ppermute(array, axis, [(i, i ^ 1 << distance) for i in range(lax.axis...  46.6 us
    all_to_all x1, waiting for transfers between devices, on_device(): lax.all_to_all(values, 'head', split_axis=1, concat_axis=0, tiled=True)  17.4 us
    all_to_all x1, waiting for transfers between devices, on_device(): lax.all_to_all(outputs, 'head', split_axis=1, concat_axis=0, tiled=True)  16.8 us
    all_to_all x1, waiting for transfers between devices, on_device(): lax.all_to_all(grad_out, 'head', split_axis=1, concat_axis=0, tiled=True)  16.4 us
    all_to_all x1, waiting for transfers between devices, on_device(): lax.all_to_all(keys, 'head', split_axis=1, concat_axis=0, tiled=True)  15.9 us
    all_to_all x1, waiting for transfers between devices, on_device(): lax.all_to_all(rounded_v, 'head', split_axis=0, concat_axis=1, tiled=True)  15.1 us
    dot_general x3, matrix products, pair_terms(): jnp.einsum('qhd,khd->hqk', qb, kb, preferred_element_type=jnp.float32)  11.3 us
  transfers between devices with their start and end apart: 17, of which 9 were waited for; matrix products, arithmetic and copies ran while one was open for 21% of the time, Pallas kernels for 0%

commit v1 on v0

v1 whole, which is shorter than its diff:
```python
import functools

import jax
import jax.numpy as jnp
from jax import lax
from jax.experimental import pallas as pl
from jax.experimental.pallas import tpu as pltpu
from jax.sharding import PartitionSpec as P

H = 32
HD = 128
RUN = 64
RUNS = 8
BLOCKS = 4
B = RUN * RUNS
LOG2E = 1.4426950408889634
SCALE = 1.0 / HD**0.5
Q, K, DO, V = 0, 1, 2, 3
NT = (((1,), (1,)), ((), ()))
NN = (((1,), (0,)), ((), ()))
TN = (((0,), (0,)), ((), ()))


def dot(a, b, dims):
    return lax.dot_general(a, b, dims, preferred_element_type=jnp.float32)


def partner(block, step):
    if step == 0:
        return block
    if step == 1:
        return (block + 2) % 4
    return block + 1 - 2 * (block % 2)


def kernel(
    ctx_size,
    live_ref,
    lse_ref,
    q_ref,
    k_ref,
    v_ref,
    o_ref,
    do_ref,
    gq_ref,
    gk_ref,
    gv_ref,
    buf,
    stat,
    stat_src,
    probs,
    grad_s,
    stage,
    rows,
    load_sem,
    send_sem,
    recv_sem,
    stat_sem,
    back_send,
    back_recv,
):
    run = lax.axis_index("head")
    ctx = lax.axis_index("ctx")
    quarter = ctx_size // 4
    rest = ctx % quarter
    block = ctx // quarter
    y_lo = block // 2
    z_hi = block % 2
    y = run // 2 * 2 + y_lo
    core = run % 2
    head = run * 4 + block
    my_columns = pl.ds(pl.multiple_of(head * HD, HD), HD)

    def peer(t):
        p = t // 4
        dy = 4 + (p % 2) * ((p + 1) // 2) - (1 - p % 2) * (p // 2)
        y_there = (y + dy) % 8
        z_there = (z_hi + 1 - t // 2 % 2) % 2
        core_there = (core + 1 - t % 2) % 2
        return y_there // 2 * 2 + core_there, y_there % 2 * 2 + z_there

    def device(run_there, block_there):
        return (run_there, block_there * quarter + rest)

    load_do = pltpu.make_async_copy(do_ref, rows.at[0], load_sem.at[0])
    load_o = pltpu.make_async_copy(o_ref, rows.at[1], load_sem.at[1])
    load_do.start()
    load_o.start()

    barrier = pltpu.get_barrier_semaphore()

    def greet(t, carry):
        run_there, block_there = peer(t)
        pl.semaphore_signal(
            barrier, inc=1, device_id=device(run_there, block_there), device_id_type=pl.DeviceIdType.MESH
        )
        return carry

    lax.fori_loop(0, 31, greet, 0)
    pl.semaphore_wait(barrier, 31)

    def slot(array):
        return buf.at[array, pl.ds(pl.multiple_of((block * RUNS + run) * RUN, RUN), RUN)]

    def send_array(source, array):
        def body(t, carry):
            run_there, block_there = peer(t)
            column = pl.multiple_of((run_there * 4 + block_there) * HD, HD)
            pltpu.make_async_remote_copy(
                src_ref=source.at[:, pl.ds(column, HD)],
                dst_ref=slot(array),
                send_sem=send_sem.at[array],
                recv_sem=recv_sem.at[array],
                device_id=device(run_there, block_there),
                device_id_type=pl.DeviceIdType.MESH,
            ).start()
            return carry

        pltpu.make_async_copy(source.at[:, my_columns], slot(array), recv_sem.at[array]).start()
        lax.fori_loop(0, 31, body, 0)

    send_array(q_ref, Q)
    send_array(k_ref, K)

    load_do.wait()
    load_o.wait()
    lanes = lax.broadcasted_iota(jnp.int32, (8, HD), 1)
    half = jnp.where(lanes // RUN == run % 2, 1.0, 0.0).astype(jnp.float32)
    eye = jnp.where(
        lax.broadcasted_iota(jnp.int32, (H, H), 0) == lax.broadcasted_iota(jnp.int32, (H, H), 1), 1.0, 0.0
    ).astype(jnp.float32)
    lse = lse_ref[...]
    lse_lines = lax.dot_general(
        eye,
        jnp.concatenate([lse, lse], axis=0),
        NT,
        precision=lax.Precision.HIGHEST,
        preferred_element_type=jnp.float32,
    )
    stat_src[:, 0, :] = lse_lines * half[:1]
    ones = jnp.ones((8, 2 * HD), jnp.bfloat16)

    def delta_line(h, carry):
        columns = pl.ds(pl.multiple_of(h * HD, HD), HD)
        product = rows[0, :, columns].astype(jnp.float32) * rows[1, :, columns].astype(jnp.float32)
        high = product.astype(jnp.bfloat16)
        low = (product - high.astype(jnp.float32)).astype(jnp.bfloat16)
        both = jnp.concatenate([high, low], axis=1)
        line = dot(ones, jnp.concatenate([both, both], axis=0), NT) * half
        stat_src[h, 1:2, :] = line[:1]
        return carry

    lax.fori_loop(0, H, delta_line, 0)

    def send_stat(t, carry):
        run_there, block_there = peer(t)
        pltpu.make_async_remote_copy(
            src_ref=stat_src.at[run_there * 4 + block_there],
            dst_ref=stat.at[block * RUNS + run],
            send_sem=stat_sem.at[0],
            recv_sem=stat_sem.at[1],
            device_id=device(run_there, block_there),
            device_id_type=pl.DeviceIdType.MESH,
        ).start()
        return carry

    pltpu.make_async_copy(stat_src.at[head], stat.at[block * RUNS + run], stat_sem.at[1]).start()
    lax.fori_loop(0, 31, send_stat, 0)

    send_array(do_ref, DO)
    send_array(v_ref, V)

    def arrived(array):
        pltpu.make_async_copy(buf.at[array], buf.at[array], recv_sem.at[array]).wait()

    def rows_of(array, index):
        return buf[array, pl.ds(pl.multiple_of(index * B, B), B), :]

    def stat_line(index, which):
        parts = []
        for pair in range(RUNS // 2):
            parts.append(
                stat[index * RUNS + 2 * pair, which : which + 1, :]
                + stat[index * RUNS + 2 * pair + 1, which : which + 1, :]
            )
        return jnp.concatenate(parts, axis=1)

    arrived(Q)
    arrived(K)
    pltpu.make_async_copy(stat, stat, stat_sem.at[1]).wait()

    def probs_of(i, carry):
        line = stat_line(i, 0) * LOG2E
        queries = rows_of(Q, i)
        ctx_i = i * quarter + rest
        for step in range(3):
            offset = line
            if step > 0:
                dead = (1 - live_ref[step - 1, ctx_i]).astype(jnp.float32)
                offset = line + dead * 1e30
            keys = rows_of(K, partner(i, step))
            scores = dot(keys, queries, NT) * (SCALE * LOG2E)
            probs[i * 3 + step] = jnp.exp2(scores - offset)
        return carry

    lax.fori_loop(0, BLOCKS, probs_of, 0)

    def stage_rows(array, index):
        return stage.at[array, pl.ds(pl.multiple_of(index * B, B), B)]

    def send_back(target, array):
        def source(run_there, block_there):
            return stage.at[array, pl.ds(pl.multiple_of((block_there * RUNS + run_there) * RUN, RUN), RUN)]

        def body(t, carry):
            run_there, block_there = peer(t)
            pltpu.make_async_remote_copy(
                src_ref=source(run_there, block_there),
                dst_ref=target.at[:, my_columns],
                send_sem=back_send.at[array],
                recv_sem=back_recv.at[array],
                device_id=device(run_there, block_there),
                device_id_type=pl.DeviceIdType.MESH,
            ).start()
            return carry

        pltpu.make_async_copy(source(run, block), target.at[:, my_columns], back_recv.at[array]).start()
        lax.fori_loop(0, 31, body, 0)

    arrived(DO)

    def grad_v_of(j, carry):
        total = jnp.zeros((B, HD), jnp.float32)
        for step in range(3):
            i = partner(j, step)
            total += dot(probs[i * 3 + step].astype(jnp.bfloat16), rows_of(DO, i), NN)
        stage_rows(2, j)[...] = total.astype(jnp.bfloat16)
        return carry

    lax.fori_loop(0, BLOCKS, grad_v_of, 0)
    send_back(gv_ref, 2)

    arrived(V)

    def grad_k_of(j, carry):
        total = jnp.zeros((B, HD), jnp.float32)
        values = rows_of(V, j)
        for step in range(3):
            i = partner(j, step)
            grad_p = dot(values, rows_of(DO, i), NT)
            grad = (probs[i * 3 + step] * (grad_p - stat_line(i, 1))).astype(jnp.bfloat16)
            grad_s[i * 3 + step] = grad
            total += dot(grad, rows_of(Q, i), NN)
        stage_rows(1, j)[...] = (total * SCALE).astype(jnp.bfloat16)
        return carry

    lax.fori_loop(0, BLOCKS, grad_k_of, 0)
    send_back(gk_ref, 1)

    def grad_q_of(i, carry):
        total = jnp.zeros((B, HD), jnp.float32)
        for step in range(3):
            total += dot(grad_s[i * 3 + step], rows_of(K, partner(i, step)), TN)
        stage_rows(0, i)[...] = (total * SCALE).astype(jnp.bfloat16)
        return carry

    lax.fori_loop(0, BLOCKS, grad_q_of, 0)
    send_back(gq_ref, 0)

    sent = pl.ds(0, 31 * RUN)
    for array in range(4):
        pltpu.make_async_copy(buf.at[array, sent], buf.at[array, sent], send_sem.at[array]).wait()
    pltpu.make_async_copy(stat.at[pl.ds(0, 31)], stat.at[pl.ds(0, 31)], stat_sem.at[0]).wait()
    for array in range(3):
        pltpu.make_async_copy(stage.at[array, sent], stage.at[array, sent], back_send.at[array]).wait()
    for array, target in enumerate((gq_ref, gk_ref, gv_ref)):
        pltpu.make_async_copy(target, target, back_recv.at[array]).wait()


def on_device(queries, keys, values, outputs, grad_out, log_totals, pair_live):
    anywhere = pl.BlockSpec(memory_space=pl.ANY)
    rows = B * BLOCKS
    out = jax.ShapeDtypeStruct(queries.shape, jnp.bfloat16)
    pairs = 3 * BLOCKS
    flops = 10 * pairs * B * B * HD
    return pl.pallas_call(
        functools.partial(kernel, lax.axis_size("ctx")),
        out_shape=(out, out, out),
        in_specs=[
            pl.BlockSpec(memory_space=pltpu.SMEM),
            pl.BlockSpec(memory_space=pltpu.VMEM),
            anywhere,
            anywhere,
            anywhere,
            anywhere,
            anywhere,
        ],
        out_specs=(anywhere, anywhere, anywhere),
        scratch_shapes=[
            pltpu.VMEM((4, rows, HD), jnp.bfloat16),
            pltpu.VMEM((BLOCKS * RUNS, 2, HD), jnp.float32),
            pltpu.VMEM((H, 2, HD), jnp.float32),
            pltpu.VMEM((pairs, B, B), jnp.float32),
            pltpu.VMEM((pairs, B, B), jnp.bfloat16),
            pltpu.VMEM((3, rows, HD), jnp.bfloat16),
            pltpu.VMEM((2, RUN, H * HD), jnp.bfloat16),
            pltpu.SemaphoreType.DMA((2,)),
            pltpu.SemaphoreType.DMA((4,)),
            pltpu.SemaphoreType.DMA((4,)),
            pltpu.SemaphoreType.DMA((2,)),
            pltpu.SemaphoreType.DMA((3,)),
            pltpu.SemaphoreType.DMA((3,)),
        ],
        compiler_params=pltpu.CompilerParams(
            collective_id=0, has_side_effects=True, vmem_limit_bytes=48 * 1024 * 1024
        ),
        cost_estimate=pl.CostEstimate(
            flops=flops, bytes_accessed=8 * RUN * H * HD * 2, transcendentals=pairs * B * B
        ),
        name="pair_attention_backward",
    )(pair_live, log_totals, queries, keys, values, outputs, grad_out)


def solution(mesh):
    rows = P(("head", "ctx"), None)
    return jax.shard_map(
        on_device,
        mesh=mesh,
        in_specs=(rows, rows, rows, rows, rows, rows, P()),
        out_specs=(rows, rows, rows),
        check_vma=False,
    )
```

time: 309 us -> 110 us (0.36)
  the two profiles are of different devices: /device:TPU:8 before, /device:TPU:1 now
where the time goes in v1:
time: 110 us
  Pallas kernels  100 us (91%)
  local copies, waits for them, and re-layouts  8.39 us (8%)
    pallas_call x1, Pallas kernels, on_device(): pl.pallas_call(functools.partial(kernel, lax.axis_size('ctx')), out_shape...  100 us
    unnamed x16, local copies, waits for them, and re-layouts  8.39 us

profile of v1, /device:TPU:1, one launch (start us, length us, event | category | flops | bytes accessed | tf_op | source)
XLA Modules:
  0.0 109.5 jit_solution(17335789052929797442)
XLA Ops:
  0.6 0.0 copy-start.5
  0.6 0.8 copy.10.lse_ref
  1.4 0.0 copy-done.5
  1.4 0.0 copy-start
  1.5 1.0 copy-done
  2.5 0.0 copy-start.1
  2.5 1.0 copy-done.1
  3.5 0.0 copy-start.2
  3.5 1.0 copy-done.2
  4.6 0.0 copy-start.3
  4.6 1.0 copy-done.3
  5.6 0.0 copy-start.4
  5.6 1.0 copy-done.4
  6.7 100.5 %pair_attention_backward.1 = (bf16[64,4096]{1,0:T(8,128)(2,1)S(1)}, bf16[64,4096]{1,0:T(8,128)(2,1)S(1)}, bf16[64,4096]{1,0:T(8,128)(2,1)S(1)}) custom-call(s32[2,64]{1,0:T(2,128)S(1)} %copy-done.5, f32[64,32]{1,0:T(8,128)S(1)} %copy.10.lse_ref, bf16[64,4096]{1,0:T(8,128)(2,1)S(1)} %copy-done, bf16[64,4096]{1,0:T(8,128)(2,1)S(1)} %copy-done.1, ...), custom_call_target="tpu_custom_call" | custom-call | flops 4026531840 | bytes 4194304 | tf_op jit(solution)/shard_map/pair_attention_backward/pallas_call | solution.py:286
  107.1 0.8 copy.14
  107.9 0.8 copy.15
  108.7 0.8 copy.16
Async XLA Ops:
  0.6 0.8 copy-start.5
  1.4 1.0 copy-start
  2.5 1.0 copy-start.1
  3.5 1.0 copy-start.2
  4.6 1.0 copy-start.3
  5.6 1.0 copy-start.4

commit v2 on v1

--- a/solution.py
+++ b/solution.py
@@ -42,9 +42,7 @@
     v_ref,
     o_ref,
     do_ref,
-    gq_ref,
-    gk_ref,
-    gv_ref,
+    out_ref,
     buf,
     stat,
     stat_src,
@@ -52,6 +50,7 @@
     grad_s,
     stage,
     rows,
+    lse_rows,
     load_sem,
     send_sem,
     recv_sem,
@@ -84,8 +83,10 @@
 
     load_do = pltpu.make_async_copy(do_ref, rows.at[0], load_sem.at[0])
     load_o = pltpu.make_async_copy(o_ref, rows.at[1], load_sem.at[1])
+    load_lse = pltpu.make_async_copy(lse_ref, lse_rows, load_sem.at[2])
     load_do.start()
     load_o.start()
+    load_lse.start()
 
     barrier = pltpu.get_barrier_semaphore()
 
@@ -124,18 +125,14 @@
 
     load_do.wait()
     load_o.wait()
+    load_lse.wait()
     lanes = lax.broadcasted_iota(jnp.int32, (8, HD), 1)
     half = jnp.where(lanes // RUN == run % 2, 1.0, 0.0).astype(jnp.float32)
-    eye = jnp.where(
-        lax.broadcasted_iota(jnp.int32, (H, H), 0) == lax.broadcasted_iota(jnp.int32, (H, H), 1), 1.0, 0.0
+    twice = jnp.where(
+        lax.broadcasted_iota(jnp.int32, (RUN, HD), 0) == lax.broadcasted_iota(jnp.int32, (RUN, HD), 1) % RUN, 1.0, 0.0
     ).astype(jnp.float32)
-    lse = lse_ref[...]
     lse_lines = lax.dot_general(
-        eye,
-        jnp.concatenate([lse, lse], axis=0),
-        NT,
-        precision=lax.Precision.HIGHEST,
-        preferred_element_type=jnp.float32,
+        lse_rows[...], twice, NN, precision=lax.Precision.HIGHEST, preferred_element_type=jnp.float32
     )
     stat_src[:, 0, :] = lse_lines * half[:1]
     ones = jnp.ones((8, 2 * HD), jnp.bfloat16)
@@ -208,7 +205,9 @@
     def stage_rows(array, index):
         return stage.at[array, pl.ds(pl.multiple_of(index * B, B), B)]
 
-    def send_back(target, array):
+    def send_back(array):
+        target = out_ref.at[array]
+
         def source(run_there, block_there):
             return stage.at[array, pl.ds(pl.multiple_of((block_there * RUNS + run_there) * RUN, RUN), RUN)]
 
@@ -238,7 +237,7 @@
         return carry
 
     lax.fori_loop(0, BLOCKS, grad_v_of, 0)
-    send_back(gv_ref, 2)
+    send_back(2)
 
     arrived(V)
 
@@ -255,7 +254,7 @@
         return carry
 
     lax.fori_loop(0, BLOCKS, grad_k_of, 0)
-    send_back(gk_ref, 1)
+    send_back(1)
 
     def grad_q_of(i, carry):
         total = jnp.zeros((B, HD), jnp.float32)
@@ -265,7 +264,7 @@
         return carry
 
     lax.fori_loop(0, BLOCKS, grad_q_of, 0)
-    send_back(gq_ref, 0)
+    send_back(0)
 
     sent = pl.ds(0, 31 * RUN)
     for array in range(4):
@@ -273,29 +272,28 @@
     pltpu.make_async_copy(stat.at[pl.ds(0, 31)], stat.at[pl.ds(0, 31)], stat_sem.at[0]).wait()
     for array in range(3):
         pltpu.make_async_copy(stage.at[array, sent], stage.at[array, sent], back_send.at[array]).wait()
-    for array, target in enumerate((gq_ref, gk_ref, gv_ref)):
-        pltpu.make_async_copy(target, target, back_recv.at[array]).wait()
+    for array in range(3):
+        pltpu.make_async_copy(out_ref.at[array], out_ref.at[array], back_recv.at[array]).wait()
 
 
 def on_device(queries, keys, values, outputs, grad_out, log_totals, pair_live):
     anywhere = pl.BlockSpec(memory_space=pl.ANY)
     rows = B * BLOCKS
-    out = jax.ShapeDtypeStruct(queries.shape, jnp.bfloat16)
     pairs = 3 * BLOCKS
     flops = 10 * pairs * B * B * HD
-    return pl.pallas_call(
+    grads = pl.pallas_call(
         functools.partial(kernel, lax.axis_size("ctx")),
-        out_shape=(out, out, out),
+        out_shape=jax.ShapeDtypeStruct((3, *queries.shape), jnp.bfloat16),
         in_specs=[
             pl.BlockSpec(memory_space=pltpu.SMEM),
-            pl.BlockSpec(memory_space=pltpu.VMEM),
+            anywhere,
             anywhere,
             anywhere,
             anywhere,
             anywhere,
             anywhere,
         ],
-        out_specs=(anywhere, anywhere, anywhere),
+        out_specs=anywhere,
         scratch_shapes=[
             pltpu.VMEM((4, rows, HD), jnp.bfloat16),
             pltpu.VMEM((BLOCKS * RUNS, 2, HD), jnp.float32),
@@ -304,7 +302,8 @@
             pltpu.VMEM((pairs, B, B), jnp.bfloat16),
             pltpu.VMEM((3, rows, HD), jnp.bfloat16),
             pltpu.VMEM((2, RUN, H * HD), jnp.bfloat16),
-            pltpu.SemaphoreType.DMA((2,)),
+            pltpu.VMEM((H, RUN), jnp.float32),
+            pltpu.SemaphoreType.DMA((3,)),
             pltpu.SemaphoreType.DMA((4,)),
             pltpu.SemaphoreType.DMA((4,)),
             pltpu.SemaphoreType.DMA((2,)),
@@ -312,13 +311,14 @@
             pltpu.SemaphoreType.DMA((3,)),
         ],
         compiler_params=pltpu.CompilerParams(
-            collective_id=0, has_side_effects=True, vmem_limit_bytes=48 * 1024 * 1024
+            collective_id=0, has_side_effects=True, vmem_limit_bytes=63 * 1024 * 1024
         ),
         cost_estimate=pl.CostEstimate(
             flops=flops, bytes_accessed=8 * RUN * H * HD * 2, transcendentals=pairs * B * B
         ),
         name="pair_attention_backward",
-    )(pair_live, log_totals, queries, keys, values, outputs, grad_out)
+    )(pair_live, jnp.transpose(log_totals), queries, keys, values, outputs, grad_out)
+    return grads[0], grads[1], grads[2]
 
 
 def solution(mesh):

time: 110 us -> 104 us (0.945)
  local copies, waits for them, and re-layouts: 8.39 us -> 2.53 us
    unnamed x16 -> x0, local copies, waits for them, and re-layouts: 8.39 us -> none
    squeeze x0 -> x1, local copies, waits for them, and re-layouts: none -> 2.53 us  [on_device(): return (grads[0], grads[1], grads[2])]
where the time goes in v2:
time: 104 us
  Pallas kernels  101 us (97%)
  local copies, waits for them, and re-layouts  2.53 us (2%)
    pallas_call x1, Pallas kernels, on_device(): pl.pallas_call(functools.partial(kernel, lax.axis_size('ctx')), out_shape...  101 us
    squeeze x1, local copies, waits for them, and re-layouts, on_device(): return (grads[0], grads[1], grads[2])  2.53 us

profile of v2, /device:TPU:1, one launch (start us, length us, event | category | flops | bytes accessed | tf_op | source)
XLA Modules:
  0.0 104.2 jit_solution(12168273584412646678)
XLA Ops:
  0.6 101.0 %pair_attention_backward.1 = bf16[3,64,4096]{2,1,0:T(8,128)(2,1)} custom-call(s32[2,64]{1,0:T(2,128)} %live_ref.1, f32[32,64]{1,0:T(8,128)} %bitcast.7, bf16[64,4096]{1,0:T(8,128)(2,1)} %q_ref.1, bf16[64,4096]{1,0:T(8,128)(2,1)} %k_ref.1, bf16[64,4096]{1,0:T(8,128)(2,1)} %v_ref.1, bf16[64,4096]{1,0:T(8,128)(2,1)} %o_ref.1, bf16[64,4096]{1,0:T(8,128)(2,1)} %do_ref.1), custom_call_target="tpu_custom_call" | custom-call | flops 4026531840 | bytes 4194304 | tf_op jit(solution)/shard_map/pair_attention_backward/pallas_call | solution.py:284
  101.7 2.5 %slice_bitcast_fusion = (bf16[64,4096]{1,0:T(8,128)(2,1)}, bf16[64,4096]{1,0:T(8,128)(2,1)}, bf16[64,4096]{1,0:T(8,128)(2,1)}) fusion(bf16[3,64,4096]{2,1,0:T(8,128)(2,1)} %pair_attention_backward.1), kind=kLoop, calls=%fused_computation | loop fusion | bytes 3145728 | tf_op jit(solution)/shard_map/squeeze | solution.py:321

commit v3 on v2

v3 whole, which is shorter than its diff:
```python
import functools

import jax
import jax.numpy as jnp
from jax import lax
from jax.experimental import pallas as pl
from jax.experimental.pallas import tpu as pltpu
from jax.sharding import PartitionSpec as P

H = 32
HD = 128
RUN = 64
RUNS = 8
BLOCKS = 4
B = RUN * RUNS
LOG2E = 1.4426950408889634
SCALE = 1.0 / HD**0.5
Q, K, DO, V = 0, 1, 2, 3
NT = (((1,), (1,)), ((), ()))
NN = (((1,), (0,)), ((), ()))
TN = (((0,), (0,)), ((), ()))


def dot(a, b, dims):
    return lax.dot_general(a, b, dims, preferred_element_type=jnp.float32)


def partner(block, step):
    if step == 0:
        return block
    if step == 1:
        return block + 1 - 2 * (block % 2)
    return (block + 2) % 4


def kernel(
    ctx_size,
    live_ref,
    lse_ref,
    q_ref,
    k_ref,
    v_ref,
    o_ref,
    do_ref,
    out_ref,
    buf,
    relay,
    stat,
    stat_src,
    stat_relay,
    probs,
    grad_s,
    stage,
    relay_back,
    rows,
    lse_rows,
    load_sem,
    send_sem,
    recv_sem,
    across_send,
    across_recv,
    stat_sem,
    back_send,
    back_recv,
    back_across_send,
    back_across_recv,
):
    run = lax.axis_index("head")
    ctx = lax.axis_index("ctx")
    quarter = ctx_size // 4
    rest = ctx % quarter
    y_lo = ctx // quarter // 2
    z_hi = ctx // quarter % 2
    y = run // 2 * 2 + y_lo
    core = run % 2
    z_other = 1 - z_hi
    block = z_hi * 2 + y_lo
    block_across = z_other * 2 + y_lo

    def head(z_there, core_there, y_there):
        return z_there * 16 + core_there * 8 + y_there

    def columns(index, count=1):
        return pl.ds(pl.multiple_of(index * HD, HD), count * HD)

    def device(y_there, core_there, z_there):
        ctx_there = (y_there % 2 * 2 + z_there) * quarter + rest
        return (y_there // 2 * 2 + core_there, ctx_there)

    def send(source, target, sent, received, where):
        pltpu.make_async_remote_copy(
            src_ref=source,
            dst_ref=target,
            send_sem=sent,
            recv_sem=received,
            device_id=where,
            device_id_type=pl.DeviceIdType.MESH,
        ).start()

    def y_at(p):
        return (y + 4 + (p % 2) * ((p + 1) // 2) - (1 - p % 2) * (p // 2)) % 8

    across = device(y, core, z_other)

    def each(first, last, body):
        lax.fori_loop(first, last, lambda t, carry: (body(t), carry)[1], 0)

    load_do = pltpu.make_async_copy(do_ref, rows.at[0], load_sem.at[0])
    load_o = pltpu.make_async_copy(o_ref, rows.at[1], load_sem.at[1])
    load_lse = pltpu.make_async_copy(lse_ref, lse_rows, load_sem.at[2])
    load_do.start()
    load_o.start()
    load_lse.start()

    barrier = pltpu.get_barrier_semaphore()

    def greet(where):
        pl.semaphore_signal(barrier, inc=1, device_id=where, device_id_type=pl.DeviceIdType.MESH)

    greet(across)
    each(0, 15, lambda t: greet(device(y_at(t // 2), (core + 1 - t % 2) % 2, z_hi)))
    pl.semaphore_wait(barrier, 16)

    def slot(array, from_block):
        return buf.at[array, pl.ds(pl.multiple_of((from_block * RUNS + run) * RUN, RUN), RUN)]

    def send_across(source, array):
        for piece in range(2):
            core_there = (core + 1 - piece) % 2
            send(
                source.at[:, columns(head(z_other, core_there, 0), 8)],
                relay.at[array, piece],
                across_send.at[0],
                across_recv.at[array * 2 + piece],
                across,
            )

    def send_column(source, array):
        def body(t):
            y_there, core_there = y_at(t // 2), (core + 1 - t % 2) % 2
            send(
                source.at[:, columns(head(z_hi, core_there, y_there))],
                slot(array, block),
                send_sem.at[array],
                recv_sem.at[array],
                device(y_there, core_there, z_hi),
            )

        mine = source.at[:, columns(head(z_hi, core, y))]
        pltpu.make_async_copy(mine, slot(array, block), recv_sem.at[array]).start()
        each(0, 15, body)

    def forward(array, piece):
        core_there = (core + 1 - piece) % 2
        arrival = relay.at[array, piece]
        pltpu.make_async_copy(arrival, arrival, across_recv.at[array * 2 + piece]).wait()

        def body(p):
            y_there = y_at(p)
            send(
                arrival.at[:, columns(y_there)],
                slot(array, block_across),
                send_sem.at[array],
                recv_sem.at[array],
                device(y_there, core_there, z_hi),
            )

        if piece == 1:
            mine = arrival.at[:, columns(y)]
            pltpu.make_async_copy(mine, slot(array, block_across), recv_sem.at[array]).start()
        each(0, 8 - piece, body)

    send_across(q_ref, Q)
    send_across(k_ref, K)
    send_column(q_ref, Q)
    send_column(k_ref, K)

    load_do.wait()
    load_o.wait()
    load_lse.wait()
    lanes = lax.broadcasted_iota(jnp.int32, (8, HD), 1)
    half = jnp.where(lanes // RUN == run % 2, 1.0, 0.0).astype(jnp.float32)
    twice = jnp.where(
        lax.broadcasted_iota(jnp.int32, (RUN, HD), 0) == lax.broadcasted_iota(jnp.int32, (RUN, HD), 1) % RUN, 1.0, 0.0
    ).astype(jnp.float32)
    lse_lines = lax.dot_general(
        lse_rows[...], twice, NN, precision=lax.Precision.HIGHEST, preferred_element_type=jnp.float32
    )
    stat_src[:, 0, :] = lse_lines * half[:1]
    ones = jnp.ones((8, 2 * HD), jnp.bfloat16)

    def delta_line(h):
        product = rows[0, :, columns(h)].astype(jnp.float32) * rows[1, :, columns(h)].astype(jnp.float32)
        high = product.astype(jnp.bfloat16)
        low = (product - high.astype(jnp.float32)).astype(jnp.bfloat16)
        both = jnp.concatenate([high, low], axis=1)
        line = dot(ones, jnp.concatenate([both, both], axis=0), NT) * half
        stat_src[h, 1:2, :] = line[:1]

    each(0, H, delta_line)

    def stat_slot(from_block):
        return stat.at[from_block * RUNS + run]

    def send_stat(source, from_block):
        def body(t):
            y_there, core_there = y_at(t // 2), (core + 1 - t % 2) % 2
            send(
                source(core_there, y_there),
                stat_slot(from_block),
                stat_sem.at[0],
                stat_sem.at[1],
                device(y_there, core_there, z_hi),
            )

        pltpu.make_async_copy(source(core, y), stat_slot(from_block), stat_sem.at[1]).start()
        each(0, 15, body)

    send(stat_src.at[pl.ds(z_other * 16, 16)], stat_relay, stat_sem.at[2], stat_sem.at[3], across)
    send_across(do_ref, DO)
    send_across(v_ref, V)
    send_stat(lambda core_there, y_there: stat_src.at[head(z_hi, core_there, y_there)], block)
    send_column(do_ref, DO)
    forward(Q, 0)
    forward(Q, 1)
    send_column(v_ref, V)
    forward(K, 0)
    forward(K, 1)
    pltpu.make_async_copy(stat_relay, stat_relay, stat_sem.at[3]).wait()
    send_stat(lambda core_there, y_there: stat_relay.at[head(0, core_there, y_there)], block_across)
    forward(DO, 0)

    def arrived(array):
        pltpu.make_async_copy(buf.at[array], buf.at[array], recv_sem.at[array]).wait()

    def rows_of(array, index):
        return buf[array, pl.ds(pl.multiple_of(index * B, B), B), :]

    def stat_line(index, which):
        parts = []
        for pair in range(RUNS // 2):
            parts.append(
                stat[index * RUNS + 2 * pair, which : which + 1, :]
                + stat[index * RUNS + 2 * pair + 1, which : which + 1, :]
            )
        return jnp.concatenate(parts, axis=1)

    arrived(Q)
    arrived(K)
    pltpu.make_async_copy(stat, stat, stat_sem.at[1]).wait()

    def probs_of(i):
        line = stat_line(i, 0) * LOG2E
        queries = rows_of(Q, i)
        ctx_i = (i % 2 * 2 + i // 2) * quarter + rest
        for step in range(3):
            offset = line
            if step > 0:
                dead = (1 - live_ref[step - 1, ctx_i]).astype(jnp.float32)
                offset = line + dead * 1e30
            keys = rows_of(K, partner(i, step))
            scores = dot(keys, queries, NT) * (SCALE * LOG2E)
            probs[i * 3 + step] = jnp.exp2(scores - offset)

    each(0, BLOCKS, probs_of)
    forward(DO, 1)
    forward(V, 0)

    def staged(array, index):
        return stage.at[array, pl.ds(pl.multiple_of(index * B, B), B)]

    def staged_run(array, index, run_there):
        return stage.at[array, pl.ds(pl.multiple_of((index * RUNS + run_there) * RUN, RUN), RUN)]

    def send_back(array):
        for piece in range(2):
            send(
                staged(array, z_other * 2 + (y_lo + piece) % 2),
                relay_back.at[array, piece],
                back_across_send.at[0],
                back_across_recv.at[array * 2 + piece],
                across,
            )
        target = out_ref.at[array, :, columns(head(z_hi, core, y))]

        def body(t):
            y_there, core_there = y_at(t // 2), (core + 1 - t % 2) % 2
            send(
                staged_run(array, z_hi * 2 + y_there % 2, y_there // 2 * 2 + core_there),
                target,
                back_send.at[array],
                back_recv.at[array],
                device(y_there, core_there, z_hi),
            )

        pltpu.make_async_copy(staged_run(array, block, run), target, back_recv.at[array]).start()
        each(0, 15, body)

    def forward_back(array, piece):
        arrival = relay_back.at[array, piece]
        pltpu.make_async_copy(arrival, arrival, back_across_recv.at[array * 2 + piece]).wait()
        target = out_ref.at[array, :, columns(head(z_other, core, y))]

        def part(run_there):
            return arrival.at[pl.ds(pl.multiple_of(run_there * RUN, RUN), RUN)]

        def body(t):
            y_there = (y + 4 + 2 * (t // 2) + piece) % 8
            core_there = (core + 1 - t % 2) % 2
            send(
                part(y_there // 2 * 2 + core_there),
                target,
                back_send.at[array],
                back_recv.at[array],
                device(y_there, core_there, z_hi),
            )

        if piece == 0:
            pltpu.make_async_copy(part(run), target, back_recv.at[array]).start()
            each(0, 5, body)
            each(6, 8, body)
        else:
            each(0, 8, body)

    arrived(DO)

    def grad_v_of(j):
        total = jnp.zeros((B, HD), jnp.float32)
        for step in range(3):
            i = partner(j, step)
            total += dot(probs[i * 3 + step].astype(jnp.bfloat16), rows_of(DO, i), NN)
        staged(2, j)[...] = total.astype(jnp.bfloat16)

    each(0, BLOCKS, grad_v_of)
    send_back(2)
    forward(V, 1)
    arrived(V)

    def grad_k_of(j):
        total = jnp.zeros((B, HD), jnp.float32)
        values = rows_of(V, j)
        for step in range(3):
            i = partner(j, step)
            grad_p = dot(values, rows_of(DO, i), NT)
            grad = (probs[i * 3 + step] * (grad_p - stat_line(i, 1))).astype(jnp.bfloat16)
            grad_s[i * 3 + step] = grad
            total += dot(grad, rows_of(Q, i), NN)
        staged(1, j)[...] = (total * SCALE).astype(jnp.bfloat16)

    each(0, BLOCKS, grad_k_of)
    send_back(1)
    forward_back(2, 0)

    def grad_q_of(i):
        total = jnp.zeros((B, HD), jnp.float32)
        for step in range(3):
            total += dot(grad_s[i * 3 + step], rows_of(K, partner(i, step)), TN)
        staged(0, i)[...] = (total * SCALE).astype(jnp.bfloat16)

    each(0, BLOCKS, grad_q_of)
    send_back(0)
    forward_back(2, 1)
    for array in (1, 0):
        for piece in range(2):
            forward_back(array, piece)

    sent = pl.ds(0, 30 * RUN)
    for array in range(4):
        pltpu.make_async_copy(buf.at[array, sent], buf.at[array, sent], send_sem.at[array]).wait()
    pltpu.make_async_copy(relay, relay, across_send.at[0]).wait()
    pltpu.make_async_copy(stat.at[pl.ds(0, 30)], stat.at[pl.ds(0, 30)], stat_sem.at[0]).wait()
    pltpu.make_async_copy(stat_relay, stat_relay, stat_sem.at[2]).wait()
    pltpu.make_async_copy(relay_back, relay_back, back_across_send.at[0]).wait()
    for array in range(3):
        pltpu.make_async_copy(stage.at[array, sent], stage.at[array, sent], back_send.at[array]).wait()
    for array in range(3):
        pltpu.make_async_copy(out_ref.at[array], out_ref.at[array], back_recv.at[array]).wait()


def on_device(queries, keys, values, outputs, grad_out, log_totals, pair_live):
    anywhere = pl.BlockSpec(memory_space=pl.ANY)
    rows = B * BLOCKS
    pairs = 3 * BLOCKS
    flops = 10 * pairs * B * B * HD
    grads = pl.pallas_call(
        functools.partial(kernel, lax.axis_size("ctx")),
        out_shape=jax.ShapeDtypeStruct((3, *queries.shape), jnp.bfloat16),
        in_specs=[
            pl.BlockSpec(memory_space=pltpu.SMEM),
            anywhere,
            anywhere,
            anywhere,
            anywhere,
            anywhere,
            anywhere,
        ],
        out_specs=anywhere,
        scratch_shapes=[
            pltpu.VMEM((4, rows, HD), jnp.bfloat16),
            pltpu.VMEM((4, 2, RUN, 8 * HD), jnp.bfloat16),
            pltpu.VMEM((BLOCKS * RUNS, 2, HD), jnp.float32),
            pltpu.VMEM((H, 2, HD), jnp.float32),
            pltpu.VMEM((H // 2, 2, HD), jnp.float32),
            pltpu.VMEM((pairs, B, B), jnp.float32),
            pltpu.VMEM((pairs, B, B), jnp.bfloat16),
            pltpu.VMEM((3, rows, HD), jnp.bfloat16),
            pltpu.VMEM((3, 2, B, HD), jnp.bfloat16),
            pltpu.VMEM((2, RUN, H * HD), jnp.bfloat16),
            pltpu.VMEM((H, RUN), jnp.float32),
            pltpu.SemaphoreType.DMA((3,)),
            pltpu.SemaphoreType.DMA((4,)),
            pltpu.SemaphoreType.DMA((4,)),
            pltpu.SemaphoreType.DMA((1,)),
            pltpu.SemaphoreType.DMA((8,)),
            pltpu.SemaphoreType.DMA((4,)),
            pltpu.SemaphoreType.DMA((3,)),
            pltpu.SemaphoreType.DMA((3,)),
            pltpu.SemaphoreType.DMA((1,)),
            pltpu.SemaphoreType.DMA((6,)),
        ],
        compiler_params=pltpu.CompilerParams(
            collective_id=0, has_side_effects=True, vmem_limit_bytes=63 * 1024 * 1024
        ),
        cost_estimate=pl.CostEstimate(
            flops=flops, bytes_accessed=8 * RUN * H * HD * 2, transcendentals=pairs * B * B
        ),
        name="pair_attention_backward",
    )(pair_live, jnp.transpose(log_totals), queries, keys, values, outputs, grad_out)
    return grads[0], grads[1], grads[2]


def solution(mesh):
    rows = P(("head", "ctx"), None)
    return jax.shard_map(
        on_device,
        mesh=mesh,
        in_specs=(rows, rows, rows, rows, rows, rows, P()),
        out_specs=(rows, rows, rows),
        check_vma=False,
    )
```

time: 104 us -> 122 us (1.17)
  the two profiles are of different devices: /device:TPU:1 before, /device:TPU:132 now
where the time goes in v3:
time: 122 us
  Pallas kernels  118 us (97%)
  local copies, waits for them, and re-layouts  2.53 us (2%)
    pallas_call x1, Pallas kernels, on_device(): pl.pallas_call(functools.partial(kernel, lax.axis_size('ctx')), out_shape...  118 us
    squeeze x1, local copies, waits for them, and re-layouts, on_device(): return (grads[0], grads[1], grads[2])  2.53 us

profile of v3, /device:TPU:132, one launch (start us, length us, event | category | flops | bytes accessed | tf_op | source)
XLA Modules:
  0.0 121.5 jit_solution(3409995217866738665)
XLA Ops:
  0.6 118.4 %pair_attention_backward.1 = bf16[3,64,4096]{2,1,0:T(8,128)(2,1)} custom-call(s32[2,64]{1,0:T(2,128)} %live_ref.1, f32[32,64]{1,0:T(8,128)} %bitcast.7, bf16[64,4096]{1,0:T(8,128)(2,1)} %q_ref.1, bf16[64,4096]{1,0:T(8,128)(2,1)} %k_ref.1, bf16[64,4096]{1,0:T(8,128)(2,1)} %v_ref.1, bf16[64,4096]{1,0:T(8,128)(2,1)} %o_ref.1, bf16[64,4096]{1,0:T(8,128)(2,1)} %do_ref.1), custom_call_target="tpu_custom_call" | custom-call | flops 4026531840 | bytes 4194304 | tf_op jit(solution)/shard_map/pair_attention_backward/pallas_call | solution.py:385
  119.0 2.5 %slice_bitcast_fusion = (bf16[64,4096]{1,0:T(8,128)(2,1)}, bf16[64,4096]{1,0:T(8,128)(2,1)}, bf16[64,4096]{1,0:T(8,128)(2,1)}) fusion(bf16[3,64,4096]{2,1,0:T(8,128)(2,1)} %pair_attention_backward.1), kind=kLoop, calls=%fused_computation | loop fusion | bytes 3145728 | tf_op jit(solution)/shard_map/squeeze | solution.py:429

commit v4 on v3

v4 whole, which is shorter than its diff:
```python
import functools

import jax
import jax.numpy as jnp
from jax import lax
from jax.experimental import pallas as pl
from jax.experimental.pallas import tpu as pltpu
from jax.sharding import PartitionSpec as P

H = 32
HD = 128
RUN = 64
RUNS = 8
BLOCKS = 4
B = RUN * RUNS
LOG2E = 1.4426950408889634
SCALE = 1.0 / HD**0.5
Q, K, DO, V = 0, 1, 2, 3
COLUMN, PARTNERS, BOTH = 0, 1, 2
NT = (((1,), (1,)), ((), ()))
NN = (((1,), (0,)), ((), ()))
TN = (((0,), (0,)), ((), ()))


def dot(a, b, dims):
    return lax.dot_general(a, b, dims, preferred_element_type=jnp.float32)


def partner(block, step):
    if step == 0:
        return block
    if step == 1:
        return block + 1 - 2 * (block % 2)
    return (block + 2) % 4


def kernel(
    ctx_size,
    live_ref,
    lse_ref,
    q_ref,
    k_ref,
    v_ref,
    o_ref,
    do_ref,
    out_ref,
    buf,
    relay,
    stat,
    stat_src,
    probs,
    grad_s,
    stage,
    rows,
    lse_rows,
    load_sem,
    send_sem,
    recv_sem,
    across_send,
    across_recv,
    stat_sem,
    back_send,
    back_recv,
):
    run = lax.axis_index("head")
    ctx = lax.axis_index("ctx")
    quarter = ctx_size // 4
    rest = ctx % quarter
    y_lo = ctx // quarter // 2
    z_hi = ctx // quarter % 2
    y = run // 2 * 2 + y_lo
    core = run % 2
    z_other = 1 - z_hi
    block = z_hi * 2 + y_lo
    block_across = z_other * 2 + y_lo

    def head(z_there, core_there, y_there):
        return z_there * 16 + core_there * 8 + y_there

    def columns(index, count=1):
        return pl.ds(pl.multiple_of(index * HD, HD), count * HD)

    def device(y_there, core_there, z_there):
        ctx_there = (y_there % 2 * 2 + z_there) * quarter + rest
        return (y_there // 2 * 2 + core_there, ctx_there)

    def send(source, target, sent, received, where):
        pltpu.make_async_remote_copy(
            src_ref=source,
            dst_ref=target,
            send_sem=sent,
            recv_sem=received,
            device_id=where,
            device_id_type=pl.DeviceIdType.MESH,
        ).start()

    def y_at(p):
        return (y + 4 + (p % 2) * ((p + 1) // 2) - (1 - p % 2) * (p // 2)) % 8

    across = device(y, core, z_other)

    def each(first, last, body):
        lax.fori_loop(first, last, lambda t, carry: (body(t), carry)[1], 0)

    barrier = pltpu.get_barrier_semaphore()

    def greet(where):
        pl.semaphore_signal(barrier, inc=1, device_id=where, device_id_type=pl.DeviceIdType.MESH)

    greet(across)
    each(0, 15, lambda t: greet(device(y_at(t // 2), (core + 1 - t % 2) % 2, z_hi)))
    load_do = pltpu.make_async_copy(do_ref, rows.at[0], load_sem.at[0])
    load_o = pltpu.make_async_copy(o_ref, rows.at[1], load_sem.at[1])
    load_lse = pltpu.make_async_copy(lse_ref, lse_rows, load_sem.at[2])
    load_do.start()
    load_o.start()
    load_lse.start()
    pl.semaphore_wait(barrier, 16)

    def slot(array, from_block):
        return buf.at[array, pl.ds(pl.multiple_of((from_block * RUNS + run) * RUN, RUN), RUN)]

    def send_across(source):
        for piece in range(2):
            core_there = (core + 1 - piece) % 2
            send(
                source.at[:, columns(head(z_other, core_there, 0), 8)],
                relay.at[piece],
                across_send.at[0],
                across_recv.at[piece],
                across,
            )

    def send_rows(source, array, reach):
        def body(t):
            if reach == BOTH:
                y_there, core_there = y_at(t // 4), (core + 1 - t % 2) % 2
                z_there = (z_hi + 1 - t // 2 % 2) % 2
            else:
                y_there, core_there = y_at(t // 2), (core + 1 - t % 2) % 2
                z_there = z_hi if reach == COLUMN else z_other
            send(
                source.at[:, columns(head(z_there, core_there, y_there))],
                slot(array, block),
                send_sem.at[array],
                recv_sem.at[array],
                device(y_there, core_there, z_there),
            )

        if reach != PARTNERS:
            mine = source.at[:, columns(head(z_hi, core, y))]
            pltpu.make_async_copy(mine, slot(array, block), recv_sem.at[array]).start()
        each(0, {COLUMN: 15, PARTNERS: 16, BOTH: 31}[reach], body)

    def forward(piece):
        core_there = (core + 1 - piece) % 2
        arrival = relay.at[piece]
        pltpu.make_async_copy(arrival, arrival, across_recv.at[piece]).wait()

        def body(p):
            y_there = y_at(p)
            send(
                arrival.at[:, columns(y_there)],
                slot(Q, block_across),
                send_sem.at[Q],
                recv_sem.at[Q],
                device(y_there, core_there, z_hi),
            )

        if piece == 1:
            pltpu.make_async_copy(arrival.at[:, columns(y)], slot(Q, block_across), recv_sem.at[Q]).start()
        each(0, 8 - piece, body)

    send_across(q_ref)
    send_rows(q_ref, Q, COLUMN)
    send_rows(k_ref, K, COLUMN)

    load_do.wait()
    load_o.wait()
    load_lse.wait()
    lanes = lax.broadcasted_iota(jnp.int32, (8, HD), 1)
    half = jnp.where(lanes // RUN == run % 2, 1.0, 0.0).astype(jnp.float32)
    twice = jnp.where(
        lax.broadcasted_iota(jnp.int32, (RUN, HD), 0) == lax.broadcasted_iota(jnp.int32, (RUN, HD), 1) % RUN, 1.0, 0.0
    ).astype(jnp.float32)
    lse_lines = lax.dot_general(
        lse_rows[...], twice, NN, precision=lax.Precision.HIGHEST, preferred_element_type=jnp.float32
    )
    stat_src[:, 0, :] = lse_lines * half[:1]
    ones = jnp.ones((8, 2 * HD), jnp.bfloat16)

    def delta_line(h):
        product = rows[0, :, columns(h)].astype(jnp.float32) * rows[1, :, columns(h)].astype(jnp.float32)
        high = product.astype(jnp.bfloat16)
        low = (product - high.astype(jnp.float32)).astype(jnp.bfloat16)
        both = jnp.concatenate([high, low], axis=1)
        line = dot(ones, jnp.concatenate([both, both], axis=0), NT) * half
        stat_src[h, 1:2, :] = line[:1]

    each(0, H, delta_line)

    forward(0)

    def send_stat(t):
        y_there, core_there = y_at(t // 4), (core + 1 - t % 2) % 2
        z_there = (z_hi + 1 - t // 2 % 2) % 2
        send(
            stat_src.at[head(z_there, core_there, y_there)],
            stat.at[block * RUNS + run],
            stat_sem.at[0],
            stat_sem.at[1],
            device(y_there, core_there, z_there),
        )

    pltpu.make_async_copy(stat_src.at[head(z_hi, core, y)], stat.at[block * RUNS + run], stat_sem.at[1]).start()
    each(0, 31, send_stat)
    send_rows(k_ref, K, PARTNERS)
    forward(1)
    send_rows(do_ref, DO, BOTH)
    send_rows(v_ref, V, BOTH)

    def arrived(array):
        pltpu.make_async_copy(buf.at[array], buf.at[array], recv_sem.at[array]).wait()

    def rows_of(array, index):
        return buf[array, pl.ds(pl.multiple_of(index * B, B), B), :]

    def stat_line(index, which):
        parts = []
        for pair in range(RUNS // 2):
            parts.append(
                stat[index * RUNS + 2 * pair, which : which + 1, :]
                + stat[index * RUNS + 2 * pair + 1, which : which + 1, :]
            )
        return jnp.concatenate(parts, axis=1)

    arrived(Q)
    arrived(K)
    pltpu.make_async_copy(stat, stat, stat_sem.at[1]).wait()

    def probs_of(i):
        line = stat_line(i, 0) * LOG2E
        queries = rows_of(Q, i)
        ctx_i = (i % 2 * 2 + i // 2) * quarter + rest
        for step in range(3):
            offset = line
            if step > 0:
                dead = (1 - live_ref[step - 1, ctx_i]).astype(jnp.float32)
                offset = line + dead * 1e30
            keys = rows_of(K, partner(i, step))
            scores = dot(keys, queries, NT) * (SCALE * LOG2E)
            probs[i * 3 + step] = jnp.exp2(scores - offset)

    each(0, BLOCKS, probs_of)

    def staged(array, index):
        return stage.at[array, pl.ds(pl.multiple_of(index * B, B), B)]

    def staged_run(array, index, run_there):
        return stage.at[array, pl.ds(pl.multiple_of((index * RUNS + run_there) * RUN, RUN), RUN)]

    def give_back(array, result_of):
        target = out_ref.at[array, :, columns(head(z_hi, core, y))]

        def one_block(t):
            z_there = (z_hi + 1 - t % 2) % 2
            odd = 1 - t // 2
            index = z_there * 2 + (y_lo + odd) % 2
            staged(array, index)[...] = result_of(index).astype(jnp.bfloat16)

            def body(u):
                q = u // 2
                y_there = y_at(4 * (q // 2) + (q % 2) * (3 - 2 * odd) + odd)
                core_there = (core + 1 - u % 2) % 2
                send(
                    staged_run(array, index, y_there // 2 * 2 + core_there),
                    target,
                    back_send.at[array],
                    back_recv.at[array],
                    device(y_there, core_there, z_there),
                )

            each(0, 8 - t // 3, body)

        each(0, BLOCKS, one_block)
        pltpu.make_async_copy(staged_run(array, block, run), target, back_recv.at[array]).start()

    arrived(DO)

    def grad_v_of(j):
        total = jnp.zeros((B, HD), jnp.float32)
        for step in range(3):
            i = partner(j, step)
            total += dot(probs[i * 3 + step].astype(jnp.bfloat16), rows_of(DO, i), NN)
        return total

    give_back(2, grad_v_of)
    arrived(V)

    def grad_k_of(j):
        total = jnp.zeros((B, HD), jnp.float32)
        values = rows_of(V, j)
        for step in range(3):
            i = partner(j, step)
            grad_p = dot(values, rows_of(DO, i), NT)
            grad = (probs[i * 3 + step] * (grad_p - stat_line(i, 1))).astype(jnp.bfloat16)
            grad_s[i * 3 + step] = grad
            total += dot(grad, rows_of(Q, i), NN)
        return total * SCALE

    give_back(1, grad_k_of)

    def grad_q_of(i):
        total = jnp.zeros((B, HD), jnp.float32)
        for step in range(3):
            total += dot(grad_s[i * 3 + step], rows_of(K, partner(i, step)), TN)
        return total * SCALE

    give_back(0, grad_q_of)

    for array in range(4):
        sent = buf.at[array, pl.ds(0, (30 if array == Q else 31) * RUN)]
        pltpu.make_async_copy(sent, sent, send_sem.at[array]).wait()
    pltpu.make_async_copy(relay, relay, across_send.at[0]).wait()
    pltpu.make_async_copy(stat.at[pl.ds(0, 31)], stat.at[pl.ds(0, 31)], stat_sem.at[0]).wait()
    for array in range(3):
        sent = stage.at[array, pl.ds(0, 31 * RUN)]
        pltpu.make_async_copy(sent, sent, back_send.at[array]).wait()
    for array in range(3):
        pltpu.make_async_copy(out_ref.at[array], out_ref.at[array], back_recv.at[array]).wait()


def on_device(queries, keys, values, outputs, grad_out, log_totals, pair_live):
    anywhere = pl.BlockSpec(memory_space=pl.ANY)
    rows = B * BLOCKS
    pairs = 3 * BLOCKS
    flops = 10 * pairs * B * B * HD
    grads = pl.pallas_call(
        functools.partial(kernel, lax.axis_size("ctx")),
        out_shape=pltpu.VMEM((3, *queries.shape), jnp.bfloat16),
        in_specs=[
            pl.BlockSpec(memory_space=pltpu.SMEM),
            anywhere,
            anywhere,
            anywhere,
            anywhere,
            anywhere,
            anywhere,
        ],
        out_specs=anywhere,
        scratch_shapes=[
            pltpu.VMEM((4, rows, HD), jnp.bfloat16),
            pltpu.VMEM((2, RUN, 8 * HD), jnp.bfloat16),
            pltpu.VMEM((BLOCKS * RUNS, 2, HD), jnp.float32),
            pltpu.VMEM((H, 2, HD), jnp.float32),
            pltpu.VMEM((pairs, B, B), jnp.float32),
            pltpu.VMEM((pairs, B, B), jnp.bfloat16),
            pltpu.VMEM((3, rows, HD), jnp.bfloat16),
            pltpu.VMEM((2, RUN, H * HD), jnp.bfloat16),
            pltpu.VMEM((H, RUN), jnp.float32),
            pltpu.SemaphoreType.DMA((3,)),
            pltpu.SemaphoreType.DMA((4,)),
            pltpu.SemaphoreType.DMA((4,)),
            pltpu.SemaphoreType.DMA((1,)),
            pltpu.SemaphoreType.DMA((2,)),
            pltpu.SemaphoreType.DMA((2,)),
            pltpu.SemaphoreType.DMA((3,)),
            pltpu.SemaphoreType.DMA((3,)),
        ],
        compiler_params=pltpu.CompilerParams(
            collective_id=0, has_side_effects=True, vmem_limit_bytes=56 * 1024 * 1024
        ),
        cost_estimate=pl.CostEstimate(
            flops=flops, bytes_accessed=8 * RUN * H * HD * 2, transcendentals=pairs * B * B
        ),
        name="pair_attention_backward",
    )(
        pair_live,
        *(
            pltpu.with_memory_space_constraint(array, pltpu.HBM)
            for array in (jnp.transpose(log_totals), queries, keys, values, outputs, grad_out)
        ),
    )
    return grads[0], grads[1], grads[2]


def solution(mesh):
    rows = P(("head", "ctx"), None)
    return jax.shard_map(
        on_device,
        mesh=mesh,
        in_specs=(rows, rows, rows, rows, rows, rows, P()),
        out_specs=(rows, rows, rows),
        check_vma=False,
    )
```

time: 122 us -> 129 us (1.057)
  the two profiles are of different devices: /device:TPU:132 before, /device:TPU:30 now
where the time goes in v4:
time: 129 us
  Pallas kernels  127 us (98%)
    pallas_call x1, Pallas kernels, on_device(): pl.pallas_call(functools.partial(kernel, lax.axis_size('ctx')), out_shape...  127 us

profile of v4, /device:TPU:30, one launch (start us, length us, event | category | flops | bytes accessed | tf_op | source)
XLA Modules:
  0.0 129.3 jit_solution(13447411567648255088)
XLA Ops:
  0.6 127.5 %pair_attention_backward.1 = bf16[3,64,4096]{2,1,0:T(8,128)(2,1)S(1)} custom-call(s32[2,64]{1,0:T(2,128)} %live_ref.1, f32[32,64]{1,0:T(8,128)} %bitcast.7, bf16[64,4096]{1,0:T(8,128)(2,1)} %q_ref.1, bf16[64,4096]{1,0:T(8,128)(2,1)} %k_ref.1, bf16[64,4096]{1,0:T(8,128)(2,1)} %v_ref.1, bf16[64,4096]{1,0:T(8,128)(2,1)} %o_ref.1, bf16[64,4096]{1,0:T(8,128)(2,1)} %do_ref.1), custom_call_target="tpu_custom_call" | custom-call | flops 4026531840 | bytes 4194304 | tf_op jit(solution)/shard_map/pair_attention_backward/pallas_call | solution.py:338
  128.1 1.2 slice_bitcast_fusion

commit v5 on v4

--- a/solution.py
+++ b/solution.py
@@ -16,7 +16,6 @@
 LOG2E = 1.4426950408889634
 SCALE = 1.0 / HD**0.5
 Q, K, DO, V = 0, 1, 2, 3
-COLUMN, PARTNERS, BOTH = 0, 1, 2
 NT = (((1,), (1,)), ((), ()))
 NN = (((1,), (0,)), ((), ()))
 TN = (((0,), (0,)), ((), ()))
@@ -45,7 +44,6 @@
     do_ref,
     out_ref,
     buf,
-    relay,
     stat,
     stat_src,
     probs,
@@ -56,8 +54,6 @@
     load_sem,
     send_sem,
     recv_sem,
-    across_send,
-    across_recv,
     stat_sem,
     back_send,
     back_recv,
@@ -70,15 +66,13 @@
     z_hi = ctx // quarter % 2
     y = run // 2 * 2 + y_lo
     core = run % 2
-    z_other = 1 - z_hi
     block = z_hi * 2 + y_lo
-    block_across = z_other * 2 + y_lo
 
     def head(z_there, core_there, y_there):
         return z_there * 16 + core_there * 8 + y_there
 
-    def columns(index, count=1):
-        return pl.ds(pl.multiple_of(index * HD, HD), count * HD)
+    def columns(index):
+        return pl.ds(pl.multiple_of(index * HD, HD), HD)
 
     def device(y_there, core_there, z_there):
         ctx_there = (y_there % 2 * 2 + z_there) * quarter + rest
@@ -97,83 +91,50 @@
     def y_at(p):
         return (y + 4 + (p % 2) * ((p + 1) // 2) - (1 - p % 2) * (p // 2)) % 8
 
-    across = device(y, core, z_other)
-
     def each(first, last, body):
         lax.fori_loop(first, last, lambda t, carry: (body(t), carry)[1], 0)
 
+    def peer(t):
+        return (core + 1 - t % 2) % 2, y_at(t // 4), (z_hi + 1 - t // 2 % 2) % 2
+
     barrier = pltpu.get_barrier_semaphore()
 
     def greet(where):
         pl.semaphore_signal(barrier, inc=1, device_id=where, device_id_type=pl.DeviceIdType.MESH)
 
-    greet(across)
-    each(0, 15, lambda t: greet(device(y_at(t // 2), (core + 1 - t % 2) % 2, z_hi)))
+    def greet_peer(t):
+        core_there, y_there, z_there = peer(t)
+        greet(device(y_there, core_there, z_there))
+
+    each(0, 31, greet_peer)
     load_do = pltpu.make_async_copy(do_ref, rows.at[0], load_sem.at[0])
     load_o = pltpu.make_async_copy(o_ref, rows.at[1], load_sem.at[1])
     load_lse = pltpu.make_async_copy(lse_ref, lse_rows, load_sem.at[2])
     load_do.start()
     load_o.start()
     load_lse.start()
-    pl.semaphore_wait(barrier, 16)
-
-    def slot(array, from_block):
-        return buf.at[array, pl.ds(pl.multiple_of((from_block * RUNS + run) * RUN, RUN), RUN)]
-
-    def send_across(source):
-        for piece in range(2):
-            core_there = (core + 1 - piece) % 2
-            send(
-                source.at[:, columns(head(z_other, core_there, 0), 8)],
-                relay.at[piece],
-                across_send.at[0],
-                across_recv.at[piece],
-                across,
-            )
-
-    def send_rows(source, array, reach):
+    pl.semaphore_wait(barrier, 31)
+
+    def slot(array):
+        return buf.at[array, pl.ds(pl.multiple_of((block * RUNS + run) * RUN, RUN), RUN)]
+
+    def send_rows(source, array):
         def body(t):
-            if reach == BOTH:
-                y_there, core_there = y_at(t // 4), (core + 1 - t % 2) % 2
-                z_there = (z_hi + 1 - t // 2 % 2) % 2
-            else:
-                y_there, core_there = y_at(t // 2), (core + 1 - t % 2) % 2
-                z_there = z_hi if reach == COLUMN else z_other
+            core_there, y_there, z_there = peer(t)
             send(
                 source.at[:, columns(head(z_there, core_there, y_there))],
-                slot(array, block),
+                slot(array),
                 send_sem.at[array],
                 recv_sem.at[array],
                 device(y_there, core_there, z_there),
             )
 
-        if reach != PARTNERS:
-            mine = source.at[:, columns(head(z_hi, core, y))]
-            pltpu.make_async_copy(mine, slot(array, block), recv_sem.at[array]).start()
-        each(0, {COLUMN: 15, PARTNERS: 16, BOTH: 31}[reach], body)
-
-    def forward(piece):
-        core_there = (core + 1 - piece) % 2
-        arrival = relay.at[piece]
-        pltpu.make_async_copy(arrival, arrival, across_recv.at[piece]).wait()
-
-        def body(p):
-            y_there = y_at(p)
-            send(
-                arrival.at[:, columns(y_there)],
-                slot(Q, block_across),
-                send_sem.at[Q],
-                recv_sem.at[Q],
-                device(y_there, core_there, z_hi),
-            )
-
-        if piece == 1:
-            pltpu.make_async_copy(arrival.at[:, columns(y)], slot(Q, block_across), recv_sem.at[Q]).start()
-        each(0, 8 - piece, body)
-
-    send_across(q_ref)
-    send_rows(q_ref, Q, COLUMN)
-    send_rows(k_ref, K, COLUMN)
+        mine = source.at[:, columns(head(z_hi, core, y))]
+        pltpu.make_async_copy(mine, slot(array), recv_sem.at[array]).start()
+        each(0, 31, body)
+
+    send_rows(q_ref, Q)
+    send_rows(k_ref, K)
 
     load_do.wait()
     load_o.wait()
@@ -199,11 +160,8 @@
 
     each(0, H, delta_line)
 
-    forward(0)
-
     def send_stat(t):
-        y_there, core_there = y_at(t // 4), (core + 1 - t % 2) % 2
-        z_there = (z_hi + 1 - t // 2 % 2) % 2
+        core_there, y_there, z_there = peer(t)
         send(
             stat_src.at[head(z_there, core_there, y_there)],
             stat.at[block * RUNS + run],
@@ -214,10 +172,8 @@
 
     pltpu.make_async_copy(stat_src.at[head(z_hi, core, y)], stat.at[block * RUNS + run], stat_sem.at[1]).start()
     each(0, 31, send_stat)
-    send_rows(k_ref, K, PARTNERS)
-    forward(1)
-    send_rows(do_ref, DO, BOTH)
-    send_rows(v_ref, V, BOTH)
+    send_rows(do_ref, DO)
+    send_rows(v_ref, V)
 
     def arrived(array):
         pltpu.make_async_copy(buf.at[array], buf.at[array], recv_sem.at[array]).wait()
@@ -319,9 +275,8 @@
     give_back(0, grad_q_of)
 
     for array in range(4):
-        sent = buf.at[array, pl.ds(0, (30 if array == Q else 31) * RUN)]
+        sent = buf.at[array, pl.ds(0, 31 * RUN)]
         pltpu.make_async_copy(sent, sent, send_sem.at[array]).wait()
-    pltpu.make_async_copy(relay, relay, across_send.at[0]).wait()
     pltpu.make_async_copy(stat.at[pl.ds(0, 31)], stat.at[pl.ds(0, 31)], stat_sem.at[0]).wait()
     for array in range(3):
         sent = stage.at[array, pl.ds(0, 31 * RUN)]
@@ -350,7 +305,6 @@
         out_specs=anywhere,
         scratch_shapes=[
             pltpu.VMEM((4, rows, HD), jnp.bfloat16),
-            pltpu.VMEM((2, RUN, 8 * HD), jnp.bfloat16),
             pltpu.VMEM((BLOCKS * RUNS, 2, HD), jnp.float32),
             pltpu.VMEM((H, 2, HD), jnp.float32),
             pltpu.VMEM((pairs, B, B), jnp.float32),
@@ -361,8 +315,6 @@
             pltpu.SemaphoreType.DMA((3,)),
             pltpu.SemaphoreType.DMA((4,)),
             pltpu.SemaphoreType.DMA((4,)),
-            pltpu.SemaphoreType.DMA((1,)),
-            pltpu.SemaphoreType.DMA((2,)),
             pltpu.SemaphoreType.DMA((2,)),
             pltpu.SemaphoreType.DMA((3,)),
             pltpu.SemaphoreType.DMA((3,)),

time: 129 us -> 103 us (0.80)
  the two profiles are of different devices: /device:TPU:30 before, /device:TPU:1 now
where the time goes in v5:
time: 103 us
  Pallas kernels  101 us (98%)
  local copies, waits for them, and re-layouts  1.17 us (1%)
    pallas_call x1, Pallas kernels, on_device(): pl.pallas_call(functools.partial(kernel, lax.axis_size('ctx')), out_shape...  101 us

profile of v5, /device:TPU:1, one launch (start us, length us, event | category | flops | bytes accessed | tf_op | source)
XLA Modules:
  0.0 103.0 jit_solution(12804772990338748415)
XLA Ops:
  0.6 101.1 %pair_attention_backward.1 = bf16[3,64,4096]{2,1,0:T(8,128)(2,1)S(1)} custom-call(s32[2,64]{1,0:T(2,128)} %live_ref.1, f32[32,64]{1,0:T(8,128)} %bitcast.7, bf16[64,4096]{1,0:T(8,128)(2,1)} %q_ref.1, bf16[64,4096]{1,0:T(8,128)(2,1)} %k_ref.1, bf16[64,4096]{1,0:T(8,128)(2,1)} %v_ref.1, bf16[64,4096]{1,0:T(8,128)(2,1)} %o_ref.1, bf16[64,4096]{1,0:T(8,128)(2,1)} %do_ref.1), custom_call_target="tpu_custom_call" | custom-call | flops 4026531840 | bytes 4194304 | tf_op jit(solution)/shard_map/pair_attention_backward/pallas_call | solution.py:293
  101.8 1.2 %slice_bitcast_fusion = (bf16[64,4096]{1,0:T(8,128)(2,1)}, bf16[64,4096]{1,0:T(8,128)(2,1)}, bf16[64,4096]{1,0:T(8,128)(2,1)}) fusion(bf16[3,64,4096]{2,1,0:T(8,128)(2,1)S(1)} %pair_attention_backward.1), kind=kLoop, calls=%fused_computation | loop fusion | bytes 3145728 | tf_op jit(solution)/shard_map/squeeze | solution.py:336

commit v6 on v5

--- a/solution.py
+++ b/solution.py
@@ -55,6 +55,7 @@
     send_sem,
     recv_sem,
     stat_sem,
+    column_sem,
     back_send,
     back_recv,
 ):
@@ -102,25 +103,35 @@
     def greet(where):
         pl.semaphore_signal(barrier, inc=1, device_id=where, device_id_type=pl.DeviceIdType.MESH)
 
+    def column_peer(t):
+        near = t // 15
+        return (core + 1 - (t + near) % 2) % 2, y_at(t // 2 - near * (t // 2 - 7)), (z_hi + near) % 2
+
+    def partners_peer(t):
+        return (core + 1 - t % 2) % 2, y_at(t // 2), 1 - z_hi
+
     def greet_peer(t):
-        core_there, y_there, z_there = peer(t)
+        core_there, y_there, z_there = column_peer(t)
         greet(device(y_there, core_there, z_there))
 
-    each(0, 31, greet_peer)
+    each(0, 17, greet_peer)
     load_do = pltpu.make_async_copy(do_ref, rows.at[0], load_sem.at[0])
     load_o = pltpu.make_async_copy(o_ref, rows.at[1], load_sem.at[1])
     load_lse = pltpu.make_async_copy(lse_ref, lse_rows, load_sem.at[2])
     load_do.start()
     load_o.start()
     load_lse.start()
-    pl.semaphore_wait(barrier, 31)
+    pl.semaphore_wait(barrier, 17)
+    pl.semaphore_signal(
+        column_sem, inc=1, device_id=device(y, core, 1 - z_hi), device_id_type=pl.DeviceIdType.MESH
+    )
 
     def slot(array):
         return buf.at[array, pl.ds(pl.multiple_of((block * RUNS + run) * RUN, RUN), RUN)]
 
-    def send_rows(source, array):
+    def send_rows(source, array, peers, count):
         def body(t):
-            core_there, y_there, z_there = peer(t)
+            core_there, y_there, z_there = peers(t)
             send(
                 source.at[:, columns(head(z_there, core_there, y_there))],
                 slot(array),
@@ -129,12 +140,19 @@
                 device(y_there, core_there, z_there),
             )
 
+        each(0, count, body)
+
+    def keep_rows(source, array):
         mine = source.at[:, columns(head(z_hi, core, y))]
         pltpu.make_async_copy(mine, slot(array), recv_sem.at[array]).start()
-        each(0, 31, body)
-
-    send_rows(q_ref, Q)
-    send_rows(k_ref, K)
+
+    send_rows(q_ref, Q, column_peer, 17)
+    send_rows(k_ref, K, column_peer, 17)
+    for array, source in ((Q, q_ref), (K, k_ref), (DO, do_ref), (V, v_ref)):
+        keep_rows(source, array)
+    pl.semaphore_wait(column_sem, 1)
+    send_rows(q_ref, Q, partners_peer, 14)
+    send_rows(k_ref, K, partners_peer, 14)
 
     load_do.wait()
     load_o.wait()
@@ -172,8 +190,8 @@
 
     pltpu.make_async_copy(stat_src.at[head(z_hi, core, y)], stat.at[block * RUNS + run], stat_sem.at[1]).start()
     each(0, 31, send_stat)
-    send_rows(do_ref, DO)
-    send_rows(v_ref, V)
+    send_rows(do_ref, DO, peer, 31)
+    send_rows(v_ref, V, peer, 31)
 
     def arrived(array):
         pltpu.make_async_copy(buf.at[array], buf.at[array], recv_sem.at[array]).wait()
@@ -316,6 +334,7 @@
             pltpu.SemaphoreType.DMA((4,)),
             pltpu.SemaphoreType.DMA((4,)),
             pltpu.SemaphoreType.DMA((2,)),
+            pltpu.SemaphoreType.REGULAR,
             pltpu.SemaphoreType.DMA((3,)),
             pltpu.SemaphoreType.DMA((3,)),
         ],

time: 103 us -> 122 us (1.18)
  the two profiles are of different devices: /device:TPU:1 before, /device:TPU:80 now
where the time goes in v6:
time: 122 us; the launch traced here: 121 us
  Pallas kernels  120 us (98%)
    pallas_call x1, Pallas kernels, on_device(): pl.pallas_call(functools.partial(kernel, lax.axis_size('ctx')), out_shape...  120 us

profile of v6, /device:TPU:80, one launch (start us, length us, event | category | flops | bytes accessed | tf_op | source)
XLA Modules:
  0.0 121.4 jit_solution(1745898837895499268)
XLA Ops:
  0.6 119.6 %pair_attention_backward.1 = bf16[3,64,4096]{2,1,0:T(8,128)(2,1)S(1)} custom-call(s32[2,64]{1,0:T(2,128)} %live_ref.1, f32[32,64]{1,0:T(8,128)} %bitcast.7, bf16[64,4096]{1,0:T(8,128)(2,1)} %q_ref.1, bf16[64,4096]{1,0:T(8,128)(2,1)} %k_ref.1, bf16[64,4096]{1,0:T(8,128)(2,1)} %v_ref.1, bf16[64,4096]{1,0:T(8,128)(2,1)} %o_ref.1, bf16[64,4096]{1,0:T(8,128)(2,1)} %do_ref.1), custom_call_target="tpu_custom_call" | custom-call | flops 4026531840 | bytes 4194304 | tf_op jit(solution)/shard_map/pair_attention_backward/pallas_call | solution.py:311
  120.3 1.2 slice_bitcast_fusion

commit v7 on v5

--- a/solution.py
+++ b/solution.py
@@ -89,13 +89,17 @@
         ).start()
 
     def y_at(p):
-        return (y + 4 + (p % 2) * ((p + 1) // 2) - (1 - p % 2) * (p // 2)) % 8
+        i = p // 2
+        return (y + 4 + i - i // 2 * (2 * i - 1) + 4 * (p % 2)) % 8
 
     def each(first, last, body):
         lax.fori_loop(first, last, lambda t, carry: (body(t), carry)[1], 0)
 
+    def place(t):
+        return (core + 1 - t % 2) % 2, y_at(t // 4), (z_hi + 1 - t // 2 % 2) % 2
+
     def peer(t):
-        return (core + 1 - t % 2) % 2, y_at(t // 4), (z_hi + 1 - t // 2 % 2) % 2
+        return place(t + (t + 24) // 31)
 
     barrier = pltpu.get_barrier_semaphore()
 
@@ -218,27 +222,30 @@
     def give_back(array, result_of):
         target = out_ref.at[array, :, columns(head(z_hi, core, y))]
 
-        def one_block(t):
-            z_there = (z_hi + 1 - t % 2) % 2
-            odd = 1 - t // 2
-            index = z_there * 2 + (y_lo + odd) % 2
-            staged(array, index)[...] = result_of(index).astype(jnp.bfloat16)
+        def half_of_blocks(t):
+            odd = 1 - t
+            y_there_lo = (y_lo + odd) % 2
+
+            def one_block(z):
+                staged(array, z * 2 + y_there_lo)[...] = result_of(z * 2 + y_there_lo).astype(jnp.bfloat16)
+
+            each(0, 2, one_block)
 
             def body(u):
-                q = u // 2
-                y_there = y_at(4 * (q // 2) + (q % 2) * (3 - 2 * odd) + odd)
-                core_there = (core + 1 - u % 2) % 2
+                v = u + t * ((u + 24) // 31)
+                q = v // 4
+                core_there, y_there, z_there = place(4 * (q + 2 * odd + t * 4 * (q // 2)) + v % 4)
                 send(
-                    staged_run(array, index, y_there // 2 * 2 + core_there),
+                    staged_run(array, z_there * 2 + y_there_lo, y_there // 2 * 2 + core_there),
                     target,
                     back_send.at[array],
                     back_recv.at[array],
                     device(y_there, core_there, z_there),
                 )
 
-            each(0, 8 - t // 3, body)
-
-        each(0, BLOCKS, one_block)
+            each(0, 16 - t, body)
+
+        each(0, 2, half_of_blocks)
         pltpu.make_async_copy(staged_run(array, block, run), target, back_recv.at[array]).start()
 
     arrived(DO)

time: 103 us -> 102 us (level)
  Pallas kernels: 101 us -> 99.8 us
    pallas_call x1, Pallas kernels: 101 us -> 99.8 us  [on_device(): pl.pallas_call(functools.partial(kernel, lax.axis_size('ctx')), out_shape...]
where the time goes in v7:
time: 102 us
  Pallas kernels  99.8 us (98%)
  local copies, waits for them, and re-layouts  1.17 us (1%)
    pallas_call x1, Pallas kernels, on_device(): pl.pallas_call(functools.partial(kernel, lax.axis_size('ctx')), out_shape...  99.8 us

profile of v7, /device:TPU:1, one launch (start us, length us, event | category | flops | bytes accessed | tf_op | source)
XLA Modules:
  0.0 101.6 jit_solution(16214764150699217207)
XLA Ops:
  0.6 99.8 %pair_attention_backward.1 = bf16[3,64,4096]{2,1,0:T(8,128)(2,1)S(1)} custom-call(s32[2,64]{1,0:T(2,128)} %live_ref.1, f32[32,64]{1,0:T(8,128)} %bitcast.7, bf16[64,4096]{1,0:T(8,128)(2,1)} %q_ref.1, bf16[64,4096]{1,0:T(8,128)(2,1)} %k_ref.1, bf16[64,4096]{1,0:T(8,128)(2,1)} %v_ref.1, bf16[64,4096]{1,0:T(8,128)(2,1)} %o_ref.1, bf16[64,4096]{1,0:T(8,128)(2,1)} %do_ref.1), custom_call_target="tpu_custom_call" | custom-call | flops 4026531840 | bytes 4194304 | tf_op jit(solution)/shard_map/pair_attention_backward/pallas_call | solution.py:300
  100.4 1.2 %slice_bitcast_fusion = (bf16[64,4096]{1,0:T(8,128)(2,1)}, bf16[64,4096]{1,0:T(8,128)(2,1)}, bf16[64,4096]{1,0:T(8,128)(2,1)}) fusion(bf16[3,64,4096]{2,1,0:T(8,128)(2,1)S(1)} %pair_attention_backward.1), kind=kLoop, calls=%fused_computation | loop fusion | bytes 3145728 | tf_op jit(solution)/shard_map/squeeze | solution.py:343

commit v8 on v7

--- a/solution.py
+++ b/solution.py
@@ -232,9 +232,9 @@
             each(0, 2, one_block)
 
             def body(u):
-                v = u + t * ((u + 24) // 31)
-                q = v // 4
-                core_there, y_there, z_there = place(4 * (q + 2 * odd + t * 4 * (q // 2)) + v % 4)
+                q = u // 4
+                q = q + t * ((q + 3) // 4 - 3 * (q // 3))
+                core_there, y_there, z_there = place(4 * (q + 2 * odd + t * 4 * (q // 2)) + u % 4)
                 send(
                     staged_run(array, z_there * 2 + y_there_lo, y_there // 2 * 2 + core_there),
                     target,
@@ -292,8 +292,18 @@
         pltpu.make_async_copy(out_ref.at[array], out_ref.at[array], back_recv.at[array]).wait()
 
 
+def store(source, *targets_and_sems):
+    *targets, sems = targets_and_sems
+    copies = [pltpu.make_async_copy(source.at[i], target, sems.at[i]) for i, target in enumerate(targets)]
+    for copy in copies:
+        copy.start()
+    for copy in copies:
+        copy.wait()
+
+
 def on_device(queries, keys, values, outputs, grad_out, log_totals, pair_live):
     anywhere = pl.BlockSpec(memory_space=pl.ANY)
+    anywhere_at_all = pl.BlockSpec(memory_space=pl.ANY)
     rows = B * BLOCKS
     pairs = 3 * BLOCKS
     flops = 10 * pairs * B * B * HD
@@ -340,7 +350,15 @@
             for array in (jnp.transpose(log_totals), queries, keys, values, outputs, grad_out)
         ),
     )
-    return grads[0], grads[1], grads[2]
+    out = jax.ShapeDtypeStruct(queries.shape, jnp.bfloat16)
+    return pl.pallas_call(
+        store,
+        out_shape=(out, out, out),
+        in_specs=[anywhere_at_all],
+        out_specs=(anywhere_at_all,) * 3,
+        scratch_shapes=[pltpu.SemaphoreType.DMA((3,))],
+        name="store_gradients",
+    )(grads)
 
 
 def solution(mesh):

time: 102 us -> 150 us (1.47)
  Pallas kernels: 99.8 us -> 148 us
    pallas_call x0 -> x1, Pallas kernels: none -> 48.8 us  [on_device(): pl.pallas_call(store, out_shape=(out, out, out), in_specs=[anywhere_at_al...]
where the time goes in v8:
time: 150 us
  Pallas kernels  148 us (99%)
    pallas_call x1, Pallas kernels, on_device(): pl.pallas_call(functools.partial(kernel, lax.axis_size('ctx')), out_shape...  99.7 us
    pallas_call x1, Pallas kernels, on_device(): pl.pallas_call(store, out_shape=(out, out, out), in_specs=[anywhere_at_al...  48.8 us

profile of v8, /device:TPU:1, one launch (start us, length us, event | category | flops | bytes accessed | tf_op | source)
XLA Modules:
  0.0 150.2 jit_solution(18388623927609246021)
XLA Ops:
  0.6 99.7 %pair_attention_backward.1.source = bf16[3,64,4096]{2,1,0:T(8,128)(2,1)S(1)} custom-call(s32[2,64]{1,0:T(2,128)} %live_ref.1, f32[32,64]{1,0:T(8,128)} %bitcast.1, bf16[64,4096]{1,0:T(8,128)(2,1)} %q_ref.1, bf16[64,4096]{1,0:T(8,128)(2,1)} %k_ref.1, bf16[64,4096]{1,0:T(8,128)(2,1)} %v_ref.1, bf16[64,4096]{1,0:T(8,128)(2,1)} %o_ref.1, bf16[64,4096]{1,0:T(8,128)(2,1)} %do_ref.1), custom_call_target="tpu_custom_call" | custom-call | flops 4026531840 | bytes 4194304 | tf_op jit(solution)/shard_map/pair_attention_backward/pallas_call | solution.py:310
  100.3 0.0 copy-start
  100.3 1.1 copy-done
  101.5 48.8 %store_gradients.1 = (bf16[64,4096]{1,0:T(8,128)(2,1)}, bf16[64,4096]{1,0:T(8,128)(2,1)}, bf16[64,4096]{1,0:T(8,128)(2,1)}) custom-call(bf16[3,64,4096]{2,1,0:T(8,128)(2,1)} %copy-done), custom_call_target="tpu_custom_call" | custom-call | tf_op jit(solution)/shard_map/store_gradients/pallas_call | solution.py:354
Async XLA Ops:
  100.3 1.2 copy-start

commit v9 on v8

--- a/solution.py
+++ b/solution.py
@@ -232,9 +232,9 @@
             each(0, 2, one_block)
 
             def body(u):
-                q = u // 4
-                q = q + t * ((q + 3) // 4 - 3 * (q // 3))
-                core_there, y_there, z_there = place(4 * (q + 2 * odd + t * 4 * (q // 2)) + u % 4)
+                v = u + t * ((u + 24) // 31)
+                q = v // 4
+                core_there, y_there, z_there = place(4 * (q + 2 * odd + t * 4 * (q // 2)) + v % 4)
                 send(
                     staged_run(array, z_there * 2 + y_there_lo, y_there // 2 * 2 + core_there),
                     target,
@@ -358,7 +358,7 @@
         out_specs=(anywhere_at_all,) * 3,
         scratch_shapes=[pltpu.SemaphoreType.DMA((3,))],
         name="store_gradients",
-    )(grads)
+    )(pltpu.with_memory_space_constraint(grads, pltpu.VMEM))
 
 
 def solution(mesh):

time: 150 us -> 102 us (0.68)
  Pallas kernels: 148 us -> 101 us
    pallas_call x1, Pallas kernels: 48.8 us -> 1.17 us  [on_device(): pl.pallas_call(store, out_shape=(out, out, out), in_specs=[anywhere_at_al...]
where the time goes in v9:
time: 102 us
  Pallas kernels  101 us (99%)
    pallas_call x1, Pallas kernels, on_device(): pl.pallas_call(functools.partial(kernel, lax.axis_size('ctx')), out_shape...  99.8 us

profile of v9, /device:TPU:1, one launch (start us, length us, event | category | flops | bytes accessed | tf_op | source)
XLA Modules:
  0.0 101.6 jit_solution(14983954386616023901)
XLA Ops:
  0.6 99.8 %pair_attention_backward.1.source = bf16[3,64,4096]{2,1,0:T(8,128)(2,1)S(1)} custom-call(s32[2,64]{1,0:T(2,128)} %live_ref.1, f32[32,64]{1,0:T(8,128)} %bitcast.1, bf16[64,4096]{1,0:T(8,128)(2,1)} %q_ref.1, bf16[64,4096]{1,0:T(8,128)(2,1)} %k_ref.1, bf16[64,4096]{1,0:T(8,128)(2,1)} %v_ref.1, bf16[64,4096]{1,0:T(8,128)(2,1)} %o_ref.1, bf16[64,4096]{1,0:T(8,128)(2,1)} %do_ref.1), custom_call_target="tpu_custom_call" | custom-call | flops 4026531840 | bytes 4194304 | tf_op jit(solution)/shard_map/pair_attention_backward/pallas_call | solution.py:310
  100.4 1.2 %store_gradients.1 = (bf16[64,4096]{1,0:T(8,128)(2,1)}, bf16[64,4096]{1,0:T(8,128)(2,1)}, bf16[64,4096]{1,0:T(8,128)(2,1)}) custom-call(bf16[3,64,4096]{2,1,0:T(8,128)(2,1)S(1)} %pair_attention_backward.1.source), custom_call_target="tpu_custom_call" | custom-call | tf_op jit(solution)/shard_map/store_gradients/pallas_call | solution.py:354
